TPU v7x, 32 devices: a whole 2x2x4 slice. The times are simulated.
32 devices in a mesh: groups: 2 (over x), side: 2 (over core), attn: 8 (over z, y).
Axes of the slice: x: 2, y: 2, z: 4, core: 2. Of those that a mesh axis runs over, the one named last changes fastest.
Arguments:
- hidden_in: bfloat16 [128, 6144], P(('groups', 'side', 'attn')), parts along dimension 0, may hold values from -24 to 24
- norm_gain: bfloat16 [6144], replicated, may hold values from 0.25 to 1.75
- routes: int32 [128, 2], P(('groups', 'side', 'attn')), parts along dimension 0, may hold values from 0 to 3, all different within a row; in each aligned block of 4 rows (0 to 3, 4 to 7, ...) at most 3 rows name the same one
- route_gates: bfloat16 [128, 2], P(('groups', 'side', 'attn')), parts along dimension 0, may hold values from 0.099609375 to 0.8984375
- w_gate: bfloat16 [6144, 40960], P(None, ('side', 'attn')), may hold values from -0.078125 to 0.078125
- w_up: bfloat16 [6144, 40960], P(None, ('side', 'attn')), may hold values from -0.078125 to 0.078125
- w_down: bfloat16 [40960, 6144], P(('side', 'attn')), may hold values from -0.0625 to 0.0625
Outputs:
- mixed: bfloat16 [128, 6144], P(('groups', 'side', 'attn')), parts along dimension 0
There are 2 independent parts, one for each index of `groups`. A program takes and returns all parts, laid end to end along the dimension named above; an argument that names none is the same for every part. Nothing has to cross between parts.
Inputs may be any that keep to these rules, and one draw needn't show every extreme that they name: `routes`: each session names 2 different experts; no expert is named by more than 3 of the rows of one device.
All inputs are finite; a program needn't handle non-finite values.
Results may differ from a plain program's by a relative error of at most 0.0065.
Values may be sent and summed in bfloat16 or wider, within the bound.
No kernel may reach another device: no remote copies, remote signals or barrier semaphores. Data moves between devices by JAX's collectives and lax.ppermute only.
A program may use at most 192 MiB of HBM per device.

v0:
```python
import jax
import jax.numpy as jnp
from jax import lax
from jax.sharding import PartitionSpec as P

EXPERTS = 4


epsilon = 1e-05


def expert_partial(inputs, w_gate, w_up, w_down):
    gate_act = jnp.dot(inputs, w_gate, preferred_element_type=jnp.float32)
    up_act = jnp.dot(inputs, w_up, preferred_element_type=jnp.float32)
    hidden = (jax.nn.silu(gate_act) * up_act).astype(jnp.bfloat16)
    return jnp.dot(hidden, w_down, preferred_element_type=jnp.float32)


def shards(hidden_in, norm_gain, routes, route_gates, w_gate, w_up, w_down):
    values = hidden_in.astype(jnp.float32)
    inverse = lax.rsqrt(jnp.mean(values * values, axis=-1, keepdims=True) + epsilon)
    normed = (values * inverse * norm_gain.astype(jnp.float32)).astype(jnp.bfloat16)
    devices = lax.axis_size(("side", "attn"))
    group_size = devices // EXPERTS
    my_expert = lax.axis_index(("side", "attn")) // group_size
    labels = jnp.arange(EXPERTS, dtype=jnp.int32)
    chosen = routes[:, :, None] == labels[None, None, :]
    coefficient = jnp.sum(
        jnp.where(chosen, route_gates[:, :, None], jnp.zeros((), jnp.bfloat16)), axis=1
    )
    all_normed, all_coeff = (
        lax.all_gather(normed, ("side", "attn"), axis=0, tiled=True),
        lax.all_gather(coefficient, ("side", "attn"), axis=0, tiled=True),
    )
    my_column = lax.dynamic_slice_in_dim(all_coeff, my_expert, 1, 1).astype(jnp.float32)
    combined = lax.psum_scatter(
        expert_partial(all_normed, w_gate, w_up, w_down) * my_column,
        ("side", "attn"),
        scatter_dimension=0,
        tiled=True,
    )
    return combined.astype(jnp.bfloat16)


def solution(mesh):
    return jax.shard_map(
        shards,
        mesh=mesh,
        in_specs=(
            P(("groups", "side", "attn"), None),
            P(),
            P(("groups", "side", "attn"), None),
            P(("groups", "side", "attn"), None),
            P(None, ("side", "attn")),
            P(None, ("side", "attn")),
            P(("side", "attn"), None),
        ),
        out_specs=P(("groups", "side", "attn"), None),
        check_vma=False,
    )
```

profile of v0, /device:TPU:0, one launch (start us, length us, event | category | flops | bytes accessed | tf_op | source)
XLA Modules:
  0.0 195.5 jit_solution(12448054331785135718)
XLA Ops:
  0.0 0.8 fusion.12
  0.8 34.1 %all-gather.1 = bf16[16,4,4]{2,1,0:T(4,128)(2,1)S(1)} all-gather(bf16[1,4,4]{2,1,0:T(4,128)(2,1)S(1)} %bitcast.14), channel_id=1, replica_groups=mesh['groups'=2,'side'=2,'attn'=8] {'side','attn'}, dimensions={0}, use_global_device_ids=true | all-gather | bytes 544 | tf_op jit(solution)/shard_map/all_gather | solution.py:33
  34.9 0.1 constant_dynamic-slice_fusion
  35.0 0.1 copy.15
  35.1 0.7 convert_element_type.19
  35.8 1.0 fusion.7
  36.7 0.9 fusion.10
  37.6 34.8 %all-gather = bf16[16,4,6144]{2,1,0:T(4,128)(2,1)S(1)} all-gather(bf16[1,4,6144]{2,1,0:T(4,128)(2,1)S(1)} %fusion.10), channel_id=1, replica_groups=mesh['groups'=2,'side'=2,'attn'=8] {'side','attn'}, dimensions={0}, use_global_device_ids=true | all-gather | bytes 835584 | tf_op jit(solution)/shard_map/all_gather | solution.py:32
  72.4 0.2 reshape.13
  72.6 12.8 %fusion.14 = f32[64,2560]{1,0:T(8,128)S(1)} fusion(bf16[64,6144]{1,0:T(8,128)(2,1)S(1)} %reshape.13, bf16[6144,2560]{1,0:T(8,128)(2,1)} %param.11), kind=kOutput, calls=%fused_computation.23 | convolution fusion | flops 2013265920 | bytes 32899072 | tf_op jit(solution)/shard_map/dot_general | solution.py:13
  85.5 0.0 copy-start
  85.5 23.5 %convolution_multiply_fusion = f32[64,6144]{1,0:T(8,128)S(1)} fusion(bf16[2560,6144]{1,0:T(8,128)(2,1)} %param.13, bf16[64,6144]{1,0:T(8,128)(2,1)S(1)} %reshape.13, bf16[6144,2560]{1,0:T(8,128)(2,1)} %param.12, f32[64]{0:T(128)S(1)} %bitcast_convert_fusion, f32[64,2560]{1,0:T(8,128)S(1)} %fusion.14), kind=kOutput, calls=%fused_computation | convolution fusion | flops 4027908096 | bytes 65929472 | tf_op jit(solution)/shard_map/dot_general | solution.py:16
  108.9 84.6 %all-reduce.2 = bf16[64,6144]{1,0:T(8,128)(2,1)S(1)} all-reduce(f32[64,6144]{1,0:T(8,128)S(1)} %convolution_multiply_fusion), channel_id=2, replica_groups=mesh['groups'=2,'side'=2,'attn'=8] {'side','attn'}, use_global_device_ids=true, to_apply=%region_2.3.clone | all-reduce | flops 393216 | bytes 2359296
  193.6 0.0 copy-done
  193.6 0.6 dynamic-slice
  194.8 0.7 dynamic-slice_convert_fusion
  (2 shorter events, 0.0 us)
Async XLA Ops:
  85.5 108.1 %copy-start = (u32[32]{0:T(128)S(1)}, u32[32]{0:T(128)}, u32[]{:S(2)}) copy-start(u32[32]{0:T(128)} %constant.47) | copy-start | bytes 388
where the time goes:
time: 196 us; the launch traced here: 195 us
  blocking collectives  154 us (79%)
  matrix products  36.3 us (19%)
  other arithmetic  3.36 us (2%)
    unnamed x1, blocking collectives  84.6 us
    all_gather x1, blocking collectives, shards(): lax.all_gather(normed, ('side', 'attn'), axis=0, tiled=True)  34.8 us
    all_gather x1, blocking collectives, shards(): lax.all_gather(coefficient, ('side', 'attn'), axis=0, tiled=True)  34.1 us
    dot_general x1, matrix products, expert_partial(): return jnp.dot(hidden, w_down, preferred_element_type=jnp.float32)  23.5 us
    dot_general x1, matrix products, expert_partial(): gate_act = jnp.dot(inputs, w_gate, preferred_element_type=jnp.float32)  12.8 us

commit v1 on v0

v1 whole, which is shorter than its diff:
```python
import jax
import jax.numpy as jnp
from jax import lax
from jax.sharding import PartitionSpec as P

EXPERTS = 4
EPSILON = 1e-05
LANES = 128


def swap_sides(values):
    sides = lax.axis_size("side")
    return lax.ppermute(values, "side", [(i, sides - 1 - i) for i in range(sides)])


def swap_chips(values, distance):
    chips = lax.axis_size("attn")
    return lax.ppermute(values, "attn", [(i, i ^ distance) for i in range(chips)])


def shards(hidden_in, norm_gain, routes, route_gates, w_gate, w_up, w_down):
    rows, width = hidden_in.shape
    chips = lax.axis_size("attn")
    devices = lax.axis_size(("side", "attn"))
    my_expert = lax.axis_index(("side", "attn")) // (devices // EXPERTS)
    values = hidden_in.astype(jnp.float32)
    inverse = lax.rsqrt(jnp.mean(values * values, axis=-1, keepdims=True) + EPSILON)
    normed = (values * inverse * norm_gain.astype(jnp.float32)).astype(jnp.bfloat16)
    labels = jnp.arange(LANES, dtype=jnp.int32)
    chosen = routes[:, :, None] == labels[None, None, :]
    coefficient = jnp.sum(
        jnp.where(chosen, route_gates[:, :, None], jnp.zeros((), jnp.bfloat16)), axis=1
    )
    payload = jnp.concatenate([normed, coefficient], axis=1)
    mine = jnp.concatenate([payload] + [swap_chips(payload, d) for d in range(1, chips)], axis=0)
    everything = jnp.concatenate([mine, swap_sides(mine)], axis=0)
    inputs = everything[:, :width]
    column = lax.dynamic_slice_in_dim(everything, width + my_expert, 1, 1).astype(jnp.float32)
    gate = jnp.dot(inputs, w_gate, preferred_element_type=jnp.float32)
    up = jnp.dot(inputs, w_up, preferred_element_type=jnp.float32)
    hidden = (jax.nn.silu(gate) * up).astype(jnp.bfloat16)
    out = jnp.dot(hidden, w_down, preferred_element_type=jnp.float32) * column
    half = rows * chips
    arrived = swap_sides(out[half:].astype(jnp.bfloat16))
    summed = (out[:half] + arrived.astype(jnp.float32)).astype(jnp.bfloat16)
    total = summed[:rows].astype(jnp.float32)
    for d in range(1, chips):
        block = swap_chips(summed[d * rows : (d + 1) * rows], d)
        total = total + block.astype(jnp.float32)
    return total.astype(jnp.bfloat16)


def solution(mesh):
    return jax.shard_map(
        shards,
        mesh=mesh,
        in_specs=(
            P(("groups", "side", "attn"), None),
            P(),
            P(("groups", "side", "attn"), None),
            P(("groups", "side", "attn"), None),
            P(None, ("side", "attn")),
            P(None, ("side", "attn")),
            P(("side", "attn"), None),
        ),
        out_specs=P(("groups", "side", "attn"), None),
        check_vma=False,
    )
```

time: 196 us -> 76.4 us (0.39)
  blocking collectives: 154 us -> 0 us
  starting transfers between devices: 0 us -> 24 us
  waiting for transfers between devices: 0 us -> 10.3 us
    unnamed x1 -> x0, blocking collectives: 84.6 us -> none
    all_gather x2 -> x0, blocking collectives: 68.9 us -> none  [the longest x1 34.8 us: shards(): lax.all_gather(normed, ('side', 'attn'), axis=0, tiled=True)]
    ppermute x0 -> x16, starting transfers between devices: none -> 24 us  [the longest x14 23.8 us: swap_chips(): lax.ppermute(values, 'attn', [(i, i ^ distance) for i in range(chips)])]
    ppermute x0 -> x16, waiting for transfers between devices: none -> 10.3 us  [the longest x14 6.99 us: swap_chips(): lax.ppermute(values, 'attn', [(i, i ^ distance) for i in range(chips)])]
  transfers between devices with their start and end apart: 0 -> 16, of which waited for: 0 -> 11; matrix products, arithmetic and copies ran while one was open for 0% -> 0% of each run, Pallas kernels for 0% -> 0%
where the time goes in v1:
time: 76.4 us; the launch traced here: 76.1 us
  matrix products  36.5 us (48%)
  starting transfers between devices  24 us (31%)
  waiting for transfers between devices  10.3 us (13%)
  other arithmetic  4.34 us (6%)
  local copies, waits for them, and re-layouts  0.91 us (1%)
    ppermute x14, starting transfers between devices, swap_chips(): lax.ppermute(values, 'attn', [(i, i ^ distance) for i in range(chips)])  23.8 us
    dot_general x1, matrix products, shards(): out = jnp.dot(hidden, w_down, preferred_element_type=jnp.float32) * column  23.7 us
    dot_general x1, matrix products, shards(): up = jnp.dot(inputs, w_up, preferred_element_type=jnp.float32)  12.8 us
    ppermute x14, waiting for transfers between devices, swap_chips(): lax.ppermute(values, 'attn', [(i, i ^ distance) for i in range(chips)])  6.99 us
    ppermute x2, waiting for transfers between devices, swap_sides(): lax.ppermute(values, 'side', [(i, sides - 1 - i) for i in range(sides)])  3.29 us
  transfers between devices with their start and end apart: 16, of which 11 were waited for; matrix products, arithmetic and copies ran while one was open for 0% of the time, Pallas kernels for 0%

profile of v1, /device:TPU:0, one launch (start us, length us, event | category | flops | bytes accessed | tf_op | source)
XLA Modules:
  0.0 76.1 jit_solution(2749469368292115293)
XLA Ops:
  0.0 1.0 %fusion.11 = f32[4]{0:T(128)S(1)} fusion(bf16[4,6144]{1,0:T(4,128)(2,1)} %param.7), kind=kLoop, calls=%fused_computation.13 | loop fusion | flops 73724 | bytes 49168 | tf_op jit(solution)/shard_map/reduce_sum | solution.py:27
  1.0 0.7 convert_element_type.50
  1.7 0.8 %fusion.15 = bf16[4,128]{1,0:T(4,128)(2,1)S(1)} fusion(s32[4,2]{0,1:T(2,128)} %param.9, bf16[4,2]{0,1:T(2,128)(2,1)} %param.10), kind=kLoop, calls=%fused_computation.21 | loop fusion | flops 2560 | bytes 1072 | tf_op jit(solution)/shard_map/reduce_sum | solution.py:31
  2.5 0.9 %fusion.13 = bf16[4,6144]{1,0:T(4,128)(2,1)S(1)} fusion(bf16[4,6144]{1,0:T(4,128)(2,1)} %param.7, f32[6144]{0:T(1024)S(1)} %convert_element_type.50, f32[4]{0:T(128)S(1)} %add_rsqrt_fusion), kind=kLoop, calls=%fused_computation.15 | loop fusion | flops 98304 | bytes 122896 | tf_op jit(solution)/shard_map/convert_element_type | solution.py:28
  3.4 6.1 %collective-permute-start.6 = (bf16[4,6272]{1,0:T(4,128)(2,1)S(1)}, bf16[4,6272]{1,0:T(4,128)(2,1)S(1)}, u32[]{:S(2)}, u32[]{:S(2)}) collective-permute-start(bf16[4,6272]{1,0:T(4,128)(2,1)S(1)} %pad_maximum_fusion), channel_id=1, source_target_pairs={{0,7},{1,6},{2,5},{3,4},{4,3},{5,2},{6,1},{7,0},{8,15},{9,14},{10,... | collective-permute-start | bytes 150536 | tf_op jit(solution)/shard_map/ppermute | solution.py:18
  9.4 0.2 collective-permute-start.5
  9.7 0.7 collective-permute-start.4
  10.4 2.0 %collective-permute-start.3 = (bf16[4,6272]{1,0:T(4,128)(2,1)S(1)}, bf16[4,6272]{1,0:T(4,128)(2,1)S(1)}, u32[]{:S(2)}, u32[]{:S(2)}) collective-permute-start(bf16[4,6272]{1,0:T(4,128)(2,1)S(1)} %pad_maximum_fusion), channel_id=1, source_target_pairs={{0,4},{1,5},{2,6},{3,7},{4,0},{5,1},{6,2},{7,3},{8,12},{9,13},{10,... | collective-permute-start | bytes 150536 | tf_op jit(solution)/shard_map/ppermute | solution.py:18
  12.5 2.3 %collective-permute-start.2 = (bf16[4,6272]{1,0:T(4,128)(2,1)S(1)}, bf16[4,6272]{1,0:T(4,128)(2,1)S(1)}, u32[]{:S(2)}, u32[]{:S(2)}) collective-permute-start(bf16[4,6272]{1,0:T(4,128)(2,1)S(1)} %pad_maximum_fusion), channel_id=1, source_target_pairs={{0,3},{1,2},{2,1},{3,0},{4,7},{5,6},{6,5},{7,4},{8,11},{9,10},{10,... | collective-permute-start | bytes 150536 | tf_op jit(solution)/shard_map/ppermute | solution.py:18
  14.7 0.0 collective-permute-done.6
  14.7 0.8 %collective-permute-start.1 = (bf16[4,6272]{1,0:T(4,128)(2,1)S(1)}, bf16[4,6272]{1,0:T(4,128)(2,1)S(1)}, u32[]{:S(2)}, u32[]{:S(2)}) collective-permute-start(bf16[4,6272]{1,0:T(4,128)(2,1)S(1)} %pad_maximum_fusion), channel_id=1, source_target_pairs={{0,2},{1,3},{2,0},{3,1},{4,6},{5,7},{6,4},{7,5},{8,10},{9,11},{10,... | collective-permute-start | bytes 150536 | tf_op jit(solution)/shard_map/ppermute | solution.py:18
  15.5 0.0 collective-permute-done.5
  15.5 0.4 collective-permute-start
  15.9 1.6 %collective-permute-done.4 = bf16[4,6272]{1,0:T(4,128)(2,1)S(1)} collective-permute-done((bf16[4,6272]{1,0:T(4,128)(2,1)S(1)}, bf16[4,6272]{1,0:T(4,128)(2,1)S(1)}, u32[]{:S(2)}, u32[]{:S(2)}) %collective-permute-start.4) | collective-permute-done | bytes 50208 | tf_op jit(solution)/shard_map/ppermute | solution.py:18
  17.5 0.2 collective-permute-done.3
  17.7 1.0 %collective-permute-done.2 = bf16[4,6272]{1,0:T(4,128)(2,1)S(1)} collective-permute-done((bf16[4,6272]{1,0:T(4,128)(2,1)S(1)}, bf16[4,6272]{1,0:T(4,128)(2,1)S(1)}, u32[]{:S(2)}, u32[]{:S(2)}) %collective-permute-start.2) | collective-permute-done | bytes 50208 | tf_op jit(solution)/shard_map/ppermute | solution.py:18
  18.7 0.1 collective-permute-done.1
  18.8 0.8 %collective-permute-done = bf16[4,6272]{1,0:T(4,128)(2,1)S(1)} collective-permute-done((bf16[4,6272]{1,0:T(4,128)(2,1)S(1)}, bf16[4,6272]{1,0:T(4,128)(2,1)S(1)}, u32[]{:S(2)}, u32[]{:S(2)}) %collective-permute-start) | collective-permute-done | bytes 50208 | tf_op jit(solution)/shard_map/ppermute | solution.py:18
  19.6 0.3 concatenate.11
  19.9 0.1 collective-permute-start.7
  20.0 1.7 %collective-permute-done.7 = bf16[32,6272]{1,0:T(8,128)(2,1)S(1)} collective-permute-done((bf16[32,6272]{1,0:T(8,128)(2,1)S(1)}, bf16[32,6272]{1,0:T(8,128)(2,1)S(1)}, u32[]{:S(2)}, u32[]{:S(2)}) %collective-permute-start.7) | collective-permute-done | bytes 401440 | tf_op jit(solution)/shard_map/ppermute | solution.py:13
  21.7 0.4 concatenate.12
  22.2 0.2 convert_reduce_fusion
  22.4 12.8 %fusion.1 = f32[64,2560]{1,0:T(8,128)S(1)} fusion(bf16[6144,2560]{1,0:T(8,128)(2,1)} %param.12, bf16[64,6272]{1,0:T(8,128)(2,1)S(1)} %concatenate.12), kind=kOutput, calls=%fused_computation.4 | convolution fusion | flops 2013265920 | bytes 32899072 | tf_op jit(solution)/shard_map/dot_general | solution.py:40
  35.2 23.7 %broadcast_multiply_fusion = f32[64,6144]{1,0:T(8,128)S(1)} fusion(f32[64]{0:T(128)S(1)} %convert_reduce_fusion, bf16[2560,6144]{1,0:T(8,128)(2,1)} %param.13, f32[64,2560]{1,0:T(8,128)S(1)} %fusion.1, bf16[6144,2560]{1,0:T(8,128)(2,1)} %param.11, bf16[64,6272]{1,0:T(8,128)(2,1)S(1)} %concatenate.12), kind=kOutput, calls=%fused_computation.3 | convolution fusion | flops 4027908096 | bytes 65929728 | tf_op jit(solution)/shard_map/dot_general | solution.py:42
  58.9 0.2 collective-permute-start.8
  59.1 1.6 %collective-permute-done.8 = bf16[32,6144]{1,0:T(8,128)(2,1)S(1)} collective-permute-done((bf16[32,6144]{1,0:T(8,128)(2,1)S(1)}, bf16[32,6144]{1,0:T(8,128)(2,1)S(1)}, u32[]{:S(2)}, u32[]{:S(2)}) %collective-permute-start.8) | collective-permute-done | bytes 393248 | tf_op jit(solution)/shard_map/ppermute | solution.py:13
  60.7 0.1 fusion
  60.7 0.1 fusion.17
  60.9 0.7 collective-permute-start.9
  61.6 4.4 %collective-permute-start.15 = (bf16[4,6144]{1,0:T(4,128)(2,1)S(1)}, bf16[4,6144]{1,0:T(4,128)(2,1)S(1)}, u32[]{:S(2)}, u32[]{:S(2)}) collective-permute-start(bf16[4,6144]{1,0:T(4,128)(2,1)S(1)} %get-tuple-element.6), channel_id=1, source_target_pairs={{0,7},{1,6},{2,5},{3,4},{4,3},{5,2},{6,1},{7,0},{8,15},{9,14},{10,... | collective-permute-start | bytes 147464 | tf_op jit(solution)/shard_map/ppermute | solution.py:18
  66.0 0.2 collective-permute-start.14
  66.2 0.4 collective-permute-start.13
  66.6 2.7 %collective-permute-start.12 = (bf16[4,6144]{1,0:T(4,128)(2,1)S(1)}, bf16[4,6144]{1,0:T(4,128)(2,1)S(1)}, u32[]{:S(2)}, u32[]{:S(2)}) collective-permute-start(bf16[4,6144]{1,0:T(4,128)(2,1)S(1)} %get-tuple-element.9), channel_id=1, source_target_pairs={{0,4},{1,5},{2,6},{3,7},{4,0},{5,1},{6,2},{7,3},{8,12},{9,13},{10,... | collective-permute-start | bytes 147464 | tf_op jit(solution)/shard_map/ppermute | solution.py:18
  69.3 0.0 collective-permute-done.9
  69.3 2.0 %collective-permute-start.11 = (bf16[4,6144]{1,0:T(4,128)(2,1)S(1)}, bf16[4,6144]{1,0:T(4,128)(2,1)S(1)}, u32[]{:S(2)}, u32[]{:S(2)}) collective-permute-start(bf16[4,6144]{1,0:T(4,128)(2,1)S(1)} %get-tuple-element.10), channel_id=1, source_target_pairs={{0,3},{1,2},{2,1},{3,0},{4,7},{5,6},{6,5},{7,4},{8,11},{9,10},{10,... | collective-permute-start | bytes 147464 | tf_op jit(solution)/shard_map/ppermute | solution.py:18
  71.3 0.0 collective-permute-done.15
  71.3 0.8 %collective-permute-start.10 = (bf16[4,6144]{1,0:T(4,128)(2,1)S(1)}, bf16[4,6144]{1,0:T(4,128)(2,1)S(1)}, u32[]{:S(2)}, u32[]{:S(2)}) collective-permute-start(bf16[4,6144]{1,0:T(4,128)(2,1)S(1)} %get-tuple-element.11), channel_id=1, source_target_pairs={{0,2},{1,3},{2,0},{3,1},{4,6},{5,7},{6,4},{7,5},{8,10},{9,11},{10,... | collective-permute-start | bytes 147464 | tf_op jit(solution)/shard_map/ppermute | solution.py:18
  72.1 0.0 collective-permute-done.14
  72.1 1.9 %collective-permute-done.13 = bf16[4,6144]{1,0:T(4,128)(2,1)S(1)} collective-permute-done((bf16[4,6144]{1,0:T(4,128)(2,1)S(1)}, bf16[4,6144]{1,0:T(4,128)(2,1)S(1)}, u32[]{:S(2)}, u32[]{:S(2)}) %collective-permute-start.13) | collective-permute-done | bytes 49184 | tf_op jit(solution)/shard_map/ppermute | solution.py:18
  74.0 0.1 collective-permute-done.12
  74.1 1.1 %collective-permute-done.11 = bf16[4,6144]{1,0:T(4,128)(2,1)S(1)} collective-permute-done((bf16[4,6144]{1,0:T(4,128)(2,1)S(1)}, bf16[4,6144]{1,0:T(4,128)(2,1)S(1)}, u32[]{:S(2)}, u32[]{:S(2)}) %collective-permute-start.11) | collective-permute-done | bytes 49184 | tf_op jit(solution)/shard_map/ppermute | solution.py:18
  75.2 0.2 collective-permute-done.10
  75.4 0.7 add_convert_fusion
  (3 shorter events, 0.1 us)
Async XLA Ops:
  3.4 11.4 %collective-permute-start.6 = (bf16[4,6272]{1,0:T(4,128)(2,1)S(1)}, bf16[4,6272]{1,0:T(4,128)(2,1)S(1)}, u32[]{:S(2)}, u32[]{:S(2)}) collective-permute-start(bf16[4,6272]{1,0:T(4,128)(2,1)S(1)} %pad_maximum_fusion), channel_id=1, source_target_pairs={{0,7},{1,6},{2,5},{3,4},{4,3},{5,2},{6,1},{7,0},{8,15},{9,14},{10,... | collective-permute-start | bytes 150536 | tf_op jit(solution)/shard_map/ppermute | solution.py:18
  9.4 6.1 %collective-permute-start.5 = (bf16[4,6272]{1,0:T(4,128)(2,1)S(1)}, bf16[4,6272]{1,0:T(4,128)(2,1)S(1)}, u32[]{:S(2)}, u32[]{:S(2)}) collective-permute-start(bf16[4,6272]{1,0:T(4,128)(2,1)S(1)} %pad_maximum_fusion), channel_id=1, source_target_pairs={{0,6},{1,7},{2,4},{3,5},{4,2},{5,3},{6,0},{7,1},{8,14},{9,15},{10,... | collective-permute-start | bytes 150536 | tf_op jit(solution)/shard_map/ppermute | solution.py:18
  9.7 7.9 %collective-permute-start.4 = (bf16[4,6272]{1,0:T(4,128)(2,1)S(1)}, bf16[4,6272]{1,0:T(4,128)(2,1)S(1)}, u32[]{:S(2)}, u32[]{:S(2)}) collective-permute-start(bf16[4,6272]{1,0:T(4,128)(2,1)S(1)} %pad_maximum_fusion), channel_id=1, source_target_pairs={{0,5},{1,4},{2,7},{3,6},{4,1},{5,0},{6,3},{7,2},{8,13},{9,12},{10,... | collective-permute-start | bytes 150536 | tf_op jit(solution)/shard_map/ppermute | solution.py:18
  10.4 7.3 %collective-permute-start.3 = (bf16[4,6272]{1,0:T(4,128)(2,1)S(1)}, bf16[4,6272]{1,0:T(4,128)(2,1)S(1)}, u32[]{:S(2)}, u32[]{:S(2)}) collective-permute-start(bf16[4,6272]{1,0:T(4,128)(2,1)S(1)} %pad_maximum_fusion), channel_id=1, source_target_pairs={{0,4},{1,5},{2,6},{3,7},{4,0},{5,1},{6,2},{7,3},{8,12},{9,13},{10,... | collective-permute-start | bytes 150536 | tf_op jit(solution)/shard_map/ppermute | solution.py:18
  12.5 6.3 %collective-permute-start.2 = (bf16[4,6272]{1,0:T(4,128)(2,1)S(1)}, bf16[4,6272]{1,0:T(4,128)(2,1)S(1)}, u32[]{:S(2)}, u32[]{:S(2)}) collective-permute-start(bf16[4,6272]{1,0:T(4,128)(2,1)S(1)} %pad_maximum_fusion), channel_id=1, source_target_pairs={{0,3},{1,2},{2,1},{3,0},{4,7},{5,6},{6,5},{7,4},{8,11},{9,10},{10,... | collective-permute-start | bytes 150536 | tf_op jit(solution)/shard_map/ppermute | solution.py:18
  14.7 4.1 %collective-permute-start.1 = (bf16[4,6272]{1,0:T(4,128)(2,1)S(1)}, bf16[4,6272]{1,0:T(4,128)(2,1)S(1)}, u32[]{:S(2)}, u32[]{:S(2)}) collective-permute-start(bf16[4,6272]{1,0:T(4,128)(2,1)S(1)} %pad_maximum_fusion), channel_id=1, source_target_pairs={{0,2},{1,3},{2,0},{3,1},{4,6},{5,7},{6,4},{7,5},{8,10},{9,11},{10,... | collective-permute-start | bytes 150536 | tf_op jit(solution)/shard_map/ppermute | solution.py:18
  15.5 4.1 %collective-permute-start = (bf16[4,6272]{1,0:T(4,128)(2,1)S(1)}, bf16[4,6272]{1,0:T(4,128)(2,1)S(1)}, u32[]{:S(2)}, u32[]{:S(2)}) collective-permute-start(bf16[4,6272]{1,0:T(4,128)(2,1)S(1)} %pad_maximum_fusion), channel_id=1, source_target_pairs={{0,1},{1,0},{2,3},{3,2},{4,5},{5,4},{6,7},{7,6},{8,9},{9,8},{10,11... | collective-permute-start | bytes 150536 | tf_op jit(solution)/shard_map/ppermute | solution.py:18
  19.9 1.8 %collective-permute-start.7 = (bf16[32,6272]{1,0:T(8,128)(2,1)S(1)}, bf16[32,6272]{1,0:T(8,128)(2,1)S(1)}, u32[]{:S(2)}, u32[]{:S(2)}) collective-permute-start(bf16[32,6272]{1,0:T(8,128)(2,1)S(1)} %concatenate.11), channel_id=1, source_target_pairs={{0,8},{8,0},{1,9},{9,1},{2,10},{10,2},{3,11},{11,3},{4,12},{12,4},... | collective-permute-start | bytes 1204232 | tf_op jit(solution)/shard_map/ppermute | solution.py:13
  58.9 1.8 %collective-permute-start.8 = (bf16[32,6144]{1,0:T(8,128)(2,1)S(1)}, bf16[32,6144]{1,0:T(8,128)(2,1)S(1)}, u32[]{:S(2)}, u32[]{:S(2)}) collective-permute-start(bf16[32,6144]{1,0:T(8,128)(2,1)S(1)} %slice.69), channel_id=1, source_target_pairs={{0,8},{8,0},{1,9},{9,1},{2,10},{10,2},{3,11},{11,3},{4,12},{12,4},... | collective-permute-start | bytes 1179656 | tf_op jit(solution)/shard_map/ppermute | solution.py:13
  60.9 8.4 %collective-permute-start.9 = (bf16[4,6144]{1,0:T(4,128)(2,1)S(1)}, bf16[4,6144]{1,0:T(4,128)(2,1)S(1)}, u32[]{:S(2)}, u32[]{:S(2)}) collective-permute-start(bf16[4,6144]{1,0:T(4,128)(2,1)S(1)} %get-tuple-element.5), channel_id=1, source_target_pairs={{0,1},{1,0},{2,3},{3,2},{4,5},{5,4},{6,7},{7,6},{8,9},{9,8},{10,11... | collective-permute-start | bytes 147464 | tf_op jit(solution)/shard_map/ppermute | solution.py:18
  61.6 9.7 %collective-permute-start.15 = (bf16[4,6144]{1,0:T(4,128)(2,1)S(1)}, bf16[4,6144]{1,0:T(4,128)(2,1)S(1)}, u32[]{:S(2)}, u32[]{:S(2)}) collective-permute-start(bf16[4,6144]{1,0:T(4,128)(2,1)S(1)} %get-tuple-element.6), channel_id=1, source_target_pairs={{0,7},{1,6},{2,5},{3,4},{4,3},{5,2},{6,1},{7,0},{8,15},{9,14},{10,... | collective-permute-start | bytes 147464 | tf_op jit(solution)/shard_map/ppermute | solution.py:18
  66.0 6.1 %collective-permute-start.14 = (bf16[4,6144]{1,0:T(4,128)(2,1)S(1)}, bf16[4,6144]{1,0:T(4,128)(2,1)S(1)}, u32[]{:S(2)}, u32[]{:S(2)}) collective-permute-start(bf16[4,6144]{1,0:T(4,128)(2,1)S(1)} %get-tuple-element.7), channel_id=1, source_target_pairs={{0,6},{1,7},{2,4},{3,5},{4,2},{5,3},{6,0},{7,1},{8,14},{9,15},{10,... | collective-permute-start | bytes 147464 | tf_op jit(solution)/shard_map/ppermute | solution.py:18
  66.2 7.8 %collective-permute-start.13 = (bf16[4,6144]{1,0:T(4,128)(2,1)S(1)}, bf16[4,6144]{1,0:T(4,128)(2,1)S(1)}, u32[]{:S(2)}, u32[]{:S(2)}) collective-permute-start(bf16[4,6144]{1,0:T(4,128)(2,1)S(1)} %get-tuple-element.8), channel_id=1, source_target_pairs={{0,5},{1,4},{2,7},{3,6},{4,1},{5,0},{6,3},{7,2},{8,13},{9,12},{10,... | collective-permute-start | bytes 147464 | tf_op jit(solution)/shard_map/ppermute | solution.py:18
  66.6 7.5 %collective-permute-start.12 = (bf16[4,6144]{1,0:T(4,128)(2,1)S(1)}, bf16[4,6144]{1,0:T(4,128)(2,1)S(1)}, u32[]{:S(2)}, u32[]{:S(2)}) collective-permute-start(bf16[4,6144]{1,0:T(4,128)(2,1)S(1)} %get-tuple-element.9), channel_id=1, source_target_pairs={{0,4},{1,5},{2,6},{3,7},{4,0},{5,1},{6,2},{7,3},{8,12},{9,13},{10,... | collective-permute-start | bytes 147464 | tf_op jit(solution)/shard_map/ppermute | solution.py:18
  69.3 5.9 %collective-permute-start.11 = (bf16[4,6144]{1,0:T(4,128)(2,1)S(1)}, bf16[4,6144]{1,0:T(4,128)(2,1)S(1)}, u32[]{:S(2)}, u32[]{:S(2)}) collective-permute-start(bf16[4,6144]{1,0:T(4,128)(2,1)S(1)} %get-tuple-element.10), channel_id=1, source_target_pairs={{0,3},{1,2},{2,1},{3,0},{4,7},{5,6},{6,5},{7,4},{8,11},{9,10},{10,... | collective-permute-start | bytes 147464 | tf_op jit(solution)/shard_map/ppermute | solution.py:18
  71.3 4.1 %collective-permute-start.10 = (bf16[4,6144]{1,0:T(4,128)(2,1)S(1)}, bf16[4,6144]{1,0:T(4,128)(2,1)S(1)}, u32[]{:S(2)}, u32[]{:S(2)}) collective-permute-start(bf16[4,6144]{1,0:T(4,128)(2,1)S(1)} %get-tuple-element.11), channel_id=1, source_target_pairs={{0,2},{1,3},{2,0},{3,1},{4,6},{5,7},{6,4},{7,5},{8,10},{9,11},{10,... | collective-permute-start | bytes 147464 | tf_op jit(solution)/shard_map/ppermute | solution.py:18

commit v2 on v1

v2 whole, which is shorter than its diff:
```python
import functools

import jax
import jax.numpy as jnp
from jax import lax
from jax.experimental import pallas as pl
from jax.experimental.pallas import tpu as pltpu
from jax.sharding import PartitionSpec as P

EXPERTS = 4
EPSILON = 1e-05
LANES = 128
MIB = 1 << 20
MIN_ROWS = 128
SLOTS = 3

VMEM = pl.BlockSpec(memory_space=pltpu.VMEM)
HBM = pl.BlockSpec(memory_space=pl.ANY)


def column_of(row_vectors, k):
    rows = row_vectors.shape[1]
    first = lax.broadcasted_iota(jnp.int32, (rows, rows), 0)
    second = lax.broadcasted_iota(jnp.int32, (rows, rows), 1)
    spread = jnp.broadcast_to(row_vectors[k : k + 1, :], (rows, rows))
    return jnp.sum(jnp.where(first == second, spread, 0.0), axis=1, keepdims=True)


def norm_kernel(hidden_ref, gain_ref, routes_ref, gates_ref, payload_ref):
    rows, width = hidden_ref.shape
    values = hidden_ref[...].astype(jnp.float32)
    inverse = lax.rsqrt(jnp.mean(values * values, axis=-1, keepdims=True) + EPSILON)
    normed = (values * inverse * gain_ref[...].astype(jnp.float32)).astype(jnp.bfloat16)
    routes = routes_ref[...].astype(jnp.float32)
    gates = gates_ref[...].astype(jnp.float32)
    labels = lax.broadcasted_iota(jnp.int32, (rows, LANES), 1).astype(jnp.float32)
    coefficient = jnp.zeros((rows, LANES), jnp.float32)
    for k in range(routes.shape[0]):
        coefficient += jnp.where(labels == column_of(routes, k), column_of(gates, k), 0.0)
    payload_ref[:, :width] = normed
    payload_ref[:, width:] = coefficient.astype(jnp.bfloat16)


def join_kernel(*refs):
    *pieces, joined = refs
    first = 0
    for piece in pieces:
        rows = piece.shape[0]
        joined[first : first + rows] = piece[...]
        first += rows


def join(pieces, vmem_bytes):
    rows = sum(piece.shape[0] for piece in pieces)
    return pl.pallas_call(
        join_kernel,
        in_specs=[VMEM] * len(pieces),
        out_specs=VMEM,
        out_shape=jax.ShapeDtypeStruct((rows, pieces[0].shape[1]), pieces[0].dtype),
        compiler_params=pltpu.CompilerParams(vmem_limit_bytes=vmem_bytes),
        name="join",
    )(*pieces)


def expert_kernel(
    devices, own_ref, other_ref, gate_ref, w_up_ref, w_down_ref,
    kept_ref, sent_ref, x, hidden, up_slots, down_slots, sems,
):
    half = own_ref.shape[0]
    rows, width = x.shape
    units = hidden.shape[1]
    up_block, down_block = up_slots.shape[2], down_slots.shape[2]
    ups = units // up_block
    downs = width // down_block
    slots = up_slots.shape[0]

    def copy(i):
        if i < ups:
            source = w_up_ref.at[:, pl.ds(i * up_block, up_block)]
            return pltpu.make_async_copy(source, up_slots.at[i % slots], sems.at[i % slots])
        j = i - ups
        source = w_down_ref.at[:, pl.ds(j * down_block, down_block)]
        return pltpu.make_async_copy(source, down_slots.at[j % slots], sems.at[slots + j % slots])

    def start(i):
        if i < ups + downs:
            copy(i).start()

    for i in range(slots):
        start(i)
    x[:half] = own_ref[:, :width]
    x[half : 2 * half] = other_ref[:, :width]
    if rows > 2 * half:
        x[2 * half :] = jnp.zeros((rows - 2 * half, width), x.dtype)

    expert = lax.axis_index(("side", "attn")) // (devices // EXPERTS)
    labels = lax.broadcasted_iota(jnp.int32, (half, LANES), 1)

    def weight_of(ref):
        tail = ref[:, width:].astype(jnp.float32)
        return jnp.sum(jnp.where(labels == expert, tail, 0.0), axis=1, keepdims=True)

    kept_weight, sent_weight = weight_of(own_ref), weight_of(other_ref)

    inputs = x[...]
    for i in range(ups):
        columns = pl.ds(i * up_block, up_block)
        gate = jnp.dot(inputs, gate_ref[:, columns], preferred_element_type=jnp.float32)
        copy(i).wait()
        up = jnp.dot(inputs, up_slots[i % slots], preferred_element_type=jnp.float32)
        start(i + slots)
        hidden[:, columns] = (gate / (1.0 + jnp.exp(-gate)) * up).astype(hidden.dtype)

    activations = hidden[...]

    def finish(weights, first, size):
        out = jnp.dot(activations, weights, preferred_element_type=jnp.float32)
        columns = pl.ds(first, size)
        kept_ref[:, columns] = (out[:half] * kept_weight).astype(kept_ref.dtype)
        sent_ref[:, columns] = (out[half : 2 * half] * sent_weight).astype(sent_ref.dtype)

    for j in range(downs):
        copy(ups + j).wait()
        finish(down_slots[j % slots], j * down_block, down_block)
        start(ups + j + slots)


def divisor(size, wanted):
    return wanted if size % wanted == 0 else size


def swap_sides(values):
    sides = lax.axis_size("side")
    return lax.ppermute(values, "side", [(i, sides - 1 - i) for i in range(sides)])


def swap_chips(values, distance):
    chips = lax.axis_size("attn")
    return lax.ppermute(values, "attn", [(i, i ^ distance) for i in range(chips)])


def shards(hidden_in, norm_gain, routes, route_gates, w_gate, w_up, w_down):
    rows, width = hidden_in.shape
    units = w_gate.shape[1]
    chips = lax.axis_size("attn")
    devices = lax.axis_size("side") * chips
    half = rows * chips
    dtype = jnp.bfloat16
    small = half <= 32
    kernel_bytes = (22 if small else 32) * MIB
    up_block, down_block = divisor(units, 256), 512

    payload = pl.pallas_call(
        norm_kernel,
        in_specs=[VMEM] * 4,
        out_specs=VMEM,
        out_shape=jax.ShapeDtypeStruct((rows, width + LANES), dtype),
        compiler_params=pltpu.CompilerParams(vmem_limit_bytes=4*MIB),
        cost_estimate=pl.CostEstimate(flops=10**11, bytes_accessed=10**6, transcendentals=0),
        name="norm",
    )(hidden_in, norm_gain.reshape(1, width), routes.T, route_gates.T)

    pair = join([payload, swap_chips(payload, 1)], 4*MIB)
    far = [swap_chips(pair, d) for d in range(2, chips, 2)]
    own = join([pair] + far, 4*MIB)
    other = swap_sides(own)

    padded = max(2 * half, MIN_ROWS)
    kept, sent = pl.pallas_call(
        functools.partial(expert_kernel, devices),
        in_specs=[VMEM] * 3 + [HBM] * 2,
        out_specs=[VMEM] * 2,
        out_shape=[jax.ShapeDtypeStruct((half, width), dtype)] * 2,
        scratch_shapes=[
            pltpu.VMEM((padded, width), dtype),
            pltpu.VMEM((padded, units), dtype),
            pltpu.VMEM((SLOTS, width, up_block), dtype),
            pltpu.VMEM((SLOTS, units, down_block), dtype),
            pltpu.SemaphoreType.DMA((2 * SLOTS,)),
        ],
        compiler_params=pltpu.CompilerParams(vmem_limit_bytes=kernel_bytes),
        cost_estimate=pl.CostEstimate(
            flops=12 * half * width * units,
            bytes_accessed=2 * units * 2 * width,
            transcendentals=2 * half * units,
        ),
        name="experts",
    )(
        own,
        other,
        pltpu.with_memory_space_constraint(w_gate, pltpu.VMEM),
        w_up,
        w_down,
    )

    def add(values):
        return sum(v.astype(jnp.float32) for v in values)

    summed = add([kept, swap_sides(sent)]).astype(dtype)
    step = 2 * rows
    arrived = [
        swap_chips(summed[d // 2 * step : (d // 2 + 1) * step], d) for d in range(2, chips, 2)
    ]
    total = add([summed[:step]] + arrived)
    return add([total[:rows], swap_chips(total[rows:].astype(dtype), 1)]).astype(dtype)


def solution(mesh):
    return jax.shard_map(
        shards,
        mesh=mesh,
        in_specs=(
            P(("groups", "side", "attn"), None),
            P(),
            P(("groups", "side", "attn"), None),
            P(("groups", "side", "attn"), None),
            P(None, ("side", "attn")),
            P(None, ("side", "attn")),
            P(("side", "attn"), None),
        ),
        out_specs=P(("groups", "side", "attn"), None),
        check_vma=False,
    )
```

time: 76.4 us -> 63 us (0.82)
  matrix products: 36.5 us -> 0 us
  Pallas kernels: 0 us -> 22.2 us
  waiting for transfers between devices: 10.3 us -> 23.6 us
  starting transfers between devices: 24 us -> 13.2 us
  other arithmetic: 4.34 us -> 0.78 us
  local copies, waits for them, and re-layouts: 0.91 us -> 2.9 us
    dot_general x2 -> x0, matrix products: 36.5 us -> none  [the longest x1 23.7 us: shards(): out = jnp.dot(hidden, w_down, preferred_element_type=jnp.float32) * column]
    pallas_call x0 -> x4, Pallas kernels: none -> 22.2 us  [the longest x1 22 us: shards(): pl.pallas_call(functools.partial(expert_kernel, devices), in_specs=[VMEM]...]
    ppermute x14 -> x8, waiting for transfers between devices: 6.99 us -> 20.3 us  [swap_chips(): lax.ppermute(values, 'attn', [(i, i ^ distance) for i in range(chips)])]
    ppermute x14 -> x8, starting transfers between devices: 23.8 us -> 13 us  [swap_chips(): lax.ppermute(values, 'attn', [(i, i ^ distance) for i in range(chips)])]
    unnamed x0 -> x8, local copies, waits for them, and re-layouts: none -> 2.13 us
    reduce_sum x2 -> x0, other arithmetic: 1.72 us -> none  [the longest x1 0.96 us: shards(): jnp.mean(values * values, axis=-1, keepdims=True) + EPSILON]
    convert_element_type x4 -> x2, other arithmetic: 2.41 us -> 0.74 us  [the longest x1 0.64 us: shards(): add([total[:rows], swap_chips(total[rows:].astype(dtype), 1)]).astype(dtype)]
  transfers between devices with their start and end apart: 16 -> 10, of which waited for: 11 -> 9; matrix products, arithmetic and copies ran while one was open for 0% -> 0% of each run, Pallas kernels for 0% -> 0%
where the time goes in v2:
time: 63 us; the launch traced here: 62.8 us
  waiting for transfers between devices  23.6 us (37%)
  Pallas kernels  22.2 us (35%)
  starting transfers between devices  13.2 us (21%)
  local copies, waits for them, and re-layouts  2.9 us (5%)
  other arithmetic  0.78 us (1%)
    pallas_call x1, Pallas kernels, shards(): pl.pallas_call(functools.partial(expert_kernel, devices), in_specs=[VMEM]...  22 us
    ppermute x8, waiting for transfers between devices, swap_chips(): lax.ppermute(values, 'attn', [(i, i ^ distance) for i in range(chips)])  20.3 us
    ppermute x8, starting transfers between devices, swap_chips(): lax.ppermute(values, 'attn', [(i, i ^ distance) for i in range(chips)])  13 us
    ppermute x2, waiting for transfers between devices, swap_sides(): lax.ppermute(values, 'side', [(i, sides - 1 - i) for i in range(sides)])  3.33 us
    unnamed x8, local copies, waits for them, and re-layouts  2.13 us
  transfers between devices with their start and end apart: 10, of which 9 were waited for; matrix products, arithmetic and copies ran while one was open for 0% of the time, Pallas kernels for 0%

profile of v2, /device:TPU:0, one launch (start us, length us, event | category | flops | bytes accessed | tf_op | source)
XLA Modules:
  0.0 62.8 jit_solution(4508279496764149011)
XLA Ops:
  0.0 0.7 %reshape.3.gain_ref = bf16[1,6144]{1,0:T(2,128)(2,1)S(1)} reshape(bf16[6144]{0:T(1024)(128)(2,1)} %param.8) | data formatting | bytes 24576 | tf_op jit(solution)/shard_map/reshape | solution.py:161
  0.7 0.0 copy-start.1
  0.7 0.8 %copy-done.1 = bf16[4,6144]{1,0:T(4,128)(2,1)S(1)} copy-done((bf16[4,6144]{1,0:T(4,128)(2,1)S(1)}, bf16[4,6144]{1,0:T(4,128)(2,1)}, u32[]{:S(2)}) %copy-start.1) | copy-done | bytes 49176
  1.5 0.0 copy-start.2
  1.5 0.7 %copy-done.2 = s32[4,2]{0,1:T(2,128)S(1)} copy-done((s32[4,2]{0,1:T(2,128)S(1)}, s32[4,2]{0,1:T(2,128)}, u32[]{:S(2)}) %copy-start.2) | copy-done | bytes 56
  2.2 0.0 copy-start.3
  2.2 0.7 %copy-done.3 = bf16[4,2]{0,1:T(2,128)(2,1)S(1)} copy-done((bf16[4,2]{0,1:T(2,128)(2,1)S(1)}, bf16[4,2]{0,1:T(2,128)(2,1)}, u32[]{:S(2)}) %copy-start.3) | copy-done | bytes 40
  2.9 0.0 copy-start
  2.9 0.2 norm.1.refs_0_
  3.0 3.0 %collective-permute-start = (bf16[4,6272]{1,0:T(4,128)(2,1)S(1)}, bf16[4,6272]{1,0:T(4,128)(2,1)S(1)}, u32[]{:S(2)}, u32[]{:S(2)}) collective-permute-start(bf16[4,6272]{1,0:T(4,128)(2,1)S(1)} %norm.1.refs_0_), channel_id=1, source_target_pairs={{0,1},{1,0},{2,3},{3,2},{4,5},{5,4},{6,7},{7,6},{8,9},{9,8},{10,11... | collective-permute-start | bytes 150536 | tf_op jit(solution)/shard_map/ppermute | solution.py:139
  6.1 2.1 %collective-permute-done.refs_1_ = bf16[4,6272]{1,0:T(4,128)(2,1)S(1)} collective-permute-done((bf16[4,6272]{1,0:T(4,128)(2,1)S(1)}, bf16[4,6272]{1,0:T(4,128)(2,1)S(1)}, u32[]{:S(2)}, u32[]{:S(2)}) %collective-permute-start) | collective-permute-done | bytes 50208 | tf_op jit(solution)/shard_map/ppermute | solution.py:139
  8.2 4.2 %collective-permute-start.3 = (bf16[8,6272]{1,0:T(8,128)(2,1)S(1)}, bf16[8,6272]{1,0:T(8,128)(2,1)S(1)}, u32[]{:S(2)}, u32[]{:S(2)}) collective-permute-start(bf16[8,6272]{1,0:T(8,128)(2,1)S(1)} %join.2.refs_0_), channel_id=1, source_target_pairs={{0,6},{1,7},{2,4},{3,5},{4,2},{5,3},{6,0},{7,1},{8,14},{9,15},{10,... | collective-permute-start | bytes 301064 | tf_op jit(solution)/shard_map/ppermute | solution.py:139
  12.3 0.0 collective-permute-start.2
  12.3 0.6 %collective-permute-start.1 = (bf16[8,6272]{1,0:T(8,128)(2,1)S(1)}, bf16[8,6272]{1,0:T(8,128)(2,1)S(1)}, u32[]{:S(2)}, u32[]{:S(2)}) collective-permute-start(bf16[8,6272]{1,0:T(8,128)(2,1)S(1)} %join.2.refs_0_), channel_id=1, source_target_pairs={{0,2},{1,3},{2,0},{3,1},{4,6},{5,7},{6,4},{7,5},{8,10},{9,11},{10,... | collective-permute-start | bytes 301064 | tf_op jit(solution)/shard_map/ppermute | solution.py:139
  13.0 2.5 %collective-permute-done.3.refs_3_ = bf16[8,6272]{1,0:T(8,128)(2,1)S(1)} collective-permute-done((bf16[8,6272]{1,0:T(8,128)(2,1)S(1)}, bf16[8,6272]{1,0:T(8,128)(2,1)S(1)}, u32[]{:S(2)}, u32[]{:S(2)}) %collective-permute-start.3) | collective-permute-done | bytes 100384 | tf_op jit(solution)/shard_map/ppermute | solution.py:139
  15.5 4.2 %collective-permute-done.2.refs_2_ = bf16[8,6272]{1,0:T(8,128)(2,1)S(1)} collective-permute-done((bf16[8,6272]{1,0:T(8,128)(2,1)S(1)}, bf16[8,6272]{1,0:T(8,128)(2,1)S(1)}, u32[]{:S(2)}, u32[]{:S(2)}) %collective-permute-start.2) | collective-permute-done | bytes 100384 | tf_op jit(solution)/shard_map/ppermute | solution.py:139
  19.7 0.0 collective-permute-done.1.refs_1_
  19.7 0.1 collective-permute-start.4
  19.8 1.7 %collective-permute-done.4.other_ref = bf16[32,6272]{1,0:T(8,128)(2,1)S(1)} collective-permute-done((bf16[32,6272]{1,0:T(8,128)(2,1)S(1)}, bf16[32,6272]{1,0:T(8,128)(2,1)S(1)}, u32[]{:S(2)}, u32[]{:S(2)}) %collective-permute-start.4) | collective-permute-done | bytes 401440 | tf_op jit(solution)/shard_map/ppermute | solution.py:134
  21.5 0.0 copy-done
  21.5 22.0 %experts.1 = (bf16[32,6144]{1,0:T(8,128)(2,1)S(1)}, bf16[32,6144]{1,0:T(8,128)(2,1)S(1)}) custom-call(bf16[32,6272]{1,0:T(8,128)(2,1)S(1)} %join.3.own_ref, bf16[32,6272]{1,0:T(8,128)(2,1)S(1)} %collective-permute-done.4.other_ref, bf16[6144,2560]{1,0:T(8,128)(2,1)S(1)} %copy-done, bf16[6144,2560]{1,0:T(8,128)(2,1)} %w_up_ref.1, bf16[2560,6144]{1,0:T(8,128)(2,1)} %w_down_ref.1), custom_call_target="tpu_custom_call" | custom-call | flops 6039797760 | bytes 62914560 | tf_op jit(solution)/shard_map/experts/pallas_call | solution.py:169
  43.5 0.2 collective-permute-start.5
  43.7 1.6 %collective-permute-done.5 = bf16[32,6144]{1,0:T(8,128)(2,1)S(1)} collective-permute-done((bf16[32,6144]{1,0:T(8,128)(2,1)S(1)}, bf16[32,6144]{1,0:T(8,128)(2,1)S(1)}, u32[]{:S(2)}, u32[]{:S(2)}) %collective-permute-start.5) | collective-permute-done | bytes 393248 | tf_op jit(solution)/shard_map/ppermute | solution.py:134
  45.3 0.1 add_convert_fusion
  45.4 0.5 collective-permute-start.6
  45.9 2.1 %collective-permute-start.8 = (bf16[8,6144]{1,0:T(8,128)(2,1)S(1)}, bf16[8,6144]{1,0:T(8,128)(2,1)S(1)}, u32[]{:S(2)}, u32[]{:S(2)}) collective-permute-start(bf16[8,6144]{1,0:T(8,128)(2,1)S(1)} %get-tuple-element.10), channel_id=1, source_target_pairs={{0,6},{1,7},{2,4},{3,5},{4,2},{5,3},{6,0},{7,1},{8,14},{9,15},{10,... | collective-permute-start | bytes 294920 | tf_op jit(solution)/shard_map/ppermute | solution.py:139
  48.0 1.0 %collective-permute-start.7 = (bf16[8,6144]{1,0:T(8,128)(2,1)S(1)}, bf16[8,6144]{1,0:T(8,128)(2,1)S(1)}, u32[]{:S(2)}, u32[]{:S(2)}) collective-permute-start(bf16[8,6144]{1,0:T(8,128)(2,1)S(1)} %get-tuple-element.11), channel_id=1, source_target_pairs={{0,4},{1,5},{2,6},{3,7},{4,0},{5,1},{6,2},{7,3},{8,12},{9,13},{10,... | collective-permute-start | bytes 294920 | tf_op jit(solution)/shard_map/ppermute | solution.py:139
  49.0 1.3 %collective-permute-done.6 = bf16[8,6144]{1,0:T(8,128)(2,1)S(1)} collective-permute-done((bf16[8,6144]{1,0:T(8,128)(2,1)S(1)}, bf16[8,6144]{1,0:T(8,128)(2,1)S(1)}, u32[]{:S(2)}, u32[]{:S(2)}) %collective-permute-start.6) | collective-permute-done | bytes 98336 | tf_op jit(solution)/shard_map/ppermute | solution.py:139
  50.3 3.4 %collective-permute-done.8 = bf16[8,6144]{1,0:T(8,128)(2,1)S(1)} collective-permute-done((bf16[8,6144]{1,0:T(8,128)(2,1)S(1)}, bf16[8,6144]{1,0:T(8,128)(2,1)S(1)}, u32[]{:S(2)}, u32[]{:S(2)}) %collective-permute-start.8) | collective-permute-done | bytes 98336 | tf_op jit(solution)/shard_map/ppermute | solution.py:139
  53.7 4.2 %collective-permute-done.7 = bf16[8,6144]{1,0:T(8,128)(2,1)S(1)} collective-permute-done((bf16[8,6144]{1,0:T(8,128)(2,1)S(1)}, bf16[8,6144]{1,0:T(8,128)(2,1)S(1)}, u32[]{:S(2)}, u32[]{:S(2)}) %collective-permute-start.7) | collective-permute-done | bytes 98336 | tf_op jit(solution)/shard_map/ppermute | solution.py:139
  58.0 1.6 %collective-permute-start.9 = (bf16[4,6144]{1,0:T(4,128)(2,1)S(1)}, bf16[4,6144]{1,0:T(4,128)(2,1)S(1)}, u32[]{:S(2)}, u32[]{:S(2)}) collective-permute-start(bf16[4,6144]{1,0:T(4,128)(2,1)S(1)} %slice.36), channel_id=1, source_target_pairs={{0,1},{1,0},{2,3},{3,2},{4,5},{5,4},{6,7},{7,6},{8,9},{9,8},{10,11... | collective-permute-start | bytes 147464 | tf_op jit(solution)/shard_map/ppermute | solution.py:139
  59.5 2.6 %collective-permute-done.9 = bf16[4,6144]{1,0:T(4,128)(2,1)S(1)} collective-permute-done((bf16[4,6144]{1,0:T(4,128)(2,1)S(1)}, bf16[4,6144]{1,0:T(4,128)(2,1)S(1)}, u32[]{:S(2)}, u32[]{:S(2)}) %collective-permute-start.9) | collective-permute-done | bytes 49184 | tf_op jit(solution)/shard_map/ppermute | solution.py:139
  62.1 0.6 %fusion = bf16[4,6144]{1,0:T(4,128)(2,1)} fusion(f32[8,6144]{1,0:T(8,128)S(1)} %convert_add_fusion, bf16[4,6144]{1,0:T(4,128)(2,1)S(1)} %collective-permute-done.9), kind=kLoop, calls=%fused_computation.4 | loop fusion | flops 73728 | bytes 196608 | tf_op jit(solution)/shard_map/convert_element_type | solution.py:205
  (5 shorter events, 0.1 us)
Async XLA Ops:
  0.7 0.8 %copy-start.1 = (bf16[4,6144]{1,0:T(4,128)(2,1)S(1)}, bf16[4,6144]{1,0:T(4,128)(2,1)}, u32[]{:S(2)}) copy-start(bf16[4,6144]{1,0:T(4,128)(2,1)} %hidden_ref.1) | copy-start | bytes 147460
  1.5 0.7 %copy-start.2 = (s32[4,2]{0,1:T(2,128)S(1)}, s32[4,2]{0,1:T(2,128)}, u32[]{:S(2)}) copy-start(s32[4,2]{0,1:T(2,128)} %param.9) | copy-start | bytes 100
  2.2 0.7 %copy-start.3 = (bf16[4,2]{0,1:T(2,128)(2,1)S(1)}, bf16[4,2]{0,1:T(2,128)(2,1)}, u32[]{:S(2)}) copy-start(bf16[4,2]{0,1:T(2,128)(2,1)} %param.10) | copy-start | bytes 52
  2.9 18.7 %copy-start = (bf16[6144,2560]{1,0:T(8,128)(2,1)S(1)}, bf16[6144,2560]{1,0:T(8,128)(2,1)}, u32[]{:S(2)}) copy-start(bf16[6144,2560]{1,0:T(8,128)(2,1)} %gate_ref.1) | copy-start | bytes 94371840
  3.0 5.1 %collective-permute-start = (bf16[4,6272]{1,0:T(4,128)(2,1)S(1)}, bf16[4,6272]{1,0:T(4,128)(2,1)S(1)}, u32[]{:S(2)}, u32[]{:S(2)}) collective-permute-start(bf16[4,6272]{1,0:T(4,128)(2,1)S(1)} %norm.1.refs_0_), channel_id=1, source_target_pairs={{0,1},{1,0},{2,3},{3,2},{4,5},{5,4},{6,7},{7,6},{8,9},{9,8},{10,11... | collective-permute-start | bytes 150536 | tf_op jit(solution)/shard_map/ppermute | solution.py:139
  8.2 7.3 %collective-permute-start.3 = (bf16[8,6272]{1,0:T(8,128)(2,1)S(1)}, bf16[8,6272]{1,0:T(8,128)(2,1)S(1)}, u32[]{:S(2)}, u32[]{:S(2)}) collective-permute-start(bf16[8,6272]{1,0:T(8,128)(2,1)S(1)} %join.2.refs_0_), channel_id=1, source_target_pairs={{0,6},{1,7},{2,4},{3,5},{4,2},{5,3},{6,0},{7,1},{8,14},{9,15},{10,... | collective-permute-start | bytes 301064 | tf_op jit(solution)/shard_map/ppermute | solution.py:139
  12.3 7.3 %collective-permute-start.2 = (bf16[8,6272]{1,0:T(8,128)(2,1)S(1)}, bf16[8,6272]{1,0:T(8,128)(2,1)S(1)}, u32[]{:S(2)}, u32[]{:S(2)}) collective-permute-start(bf16[8,6272]{1,0:T(8,128)(2,1)S(1)} %join.2.refs_0_), channel_id=1, source_target_pairs={{0,4},{1,5},{2,6},{3,7},{4,0},{5,1},{6,2},{7,3},{8,12},{9,13},{10,... | collective-permute-start | bytes 301064 | tf_op jit(solution)/shard_map/ppermute | solution.py:139
  12.3 7.3 %collective-permute-start.1 = (bf16[8,6272]{1,0:T(8,128)(2,1)S(1)}, bf16[8,6272]{1,0:T(8,128)(2,1)S(1)}, u32[]{:S(2)}, u32[]{:S(2)}) collective-permute-start(bf16[8,6272]{1,0:T(8,128)(2,1)S(1)} %join.2.refs_0_), channel_id=1, source_target_pairs={{0,2},{1,3},{2,0},{3,1},{4,6},{5,7},{6,4},{7,5},{8,10},{9,11},{10,... | collective-permute-start | bytes 301064 | tf_op jit(solution)/shard_map/ppermute | solution.py:139
  19.7 1.8 %collective-permute-start.4 = (bf16[32,6272]{1,0:T(8,128)(2,1)S(1)}, bf16[32,6272]{1,0:T(8,128)(2,1)S(1)}, u32[]{:S(2)}, u32[]{:S(2)}) collective-permute-start(bf16[32,6272]{1,0:T(8,128)(2,1)S(1)} %join.3.own_ref), channel_id=1, source_target_pairs={{0,8},{8,0},{1,9},{9,1},{2,10},{10,2},{3,11},{11,3},{4,12},{12,4},... | collective-permute-start | bytes 1204232 | tf_op jit(solution)/shard_map/ppermute | solution.py:134
  43.5 1.8 %collective-permute-start.5 = (bf16[32,6144]{1,0:T(8,128)(2,1)S(1)}, bf16[32,6144]{1,0:T(8,128)(2,1)S(1)}, u32[]{:S(2)}, u32[]{:S(2)}) collective-permute-start(bf16[32,6144]{1,0:T(8,128)(2,1)S(1)} %get-tuple-element.8), channel_id=1, source_target_pairs={{0,8},{8,0},{1,9},{9,1},{2,10},{10,2},{3,11},{11,3},{4,12},{12,4},... | collective-permute-start | bytes 1179656 | tf_op jit(solution)/shard_map/ppermute | solution.py:134
  45.4 4.9 %collective-permute-start.6 = (bf16[8,6144]{1,0:T(8,128)(2,1)S(1)}, bf16[8,6144]{1,0:T(8,128)(2,1)S(1)}, u32[]{:S(2)}, u32[]{:S(2)}) collective-permute-start(bf16[8,6144]{1,0:T(8,128)(2,1)S(1)} %get-tuple-element.9), channel_id=1, source_target_pairs={{0,2},{1,3},{2,0},{3,1},{4,6},{5,7},{6,4},{7,5},{8,10},{9,11},{10,... | collective-permute-start | bytes 294920 | tf_op jit(solution)/shard_map/ppermute | solution.py:139
  45.9 7.8 %collective-permute-start.8 = (bf16[8,6144]{1,0:T(8,128)(2,1)S(1)}, bf16[8,6144]{1,0:T(8,128)(2,1)S(1)}, u32[]{:S(2)}, u32[]{:S(2)}) collective-permute-start(bf16[8,6144]{1,0:T(8,128)(2,1)S(1)} %get-tuple-element.10), channel_id=1, source_target_pairs={{0,6},{1,7},{2,4},{3,5},{4,2},{5,3},{6,0},{7,1},{8,14},{9,15},{10,... | collective-permute-start | bytes 294920 | tf_op jit(solution)/shard_map/ppermute | solution.py:139
  48.0 9.9 %collective-permute-start.7 = (bf16[8,6144]{1,0:T(8,128)(2,1)S(1)}, bf16[8,6144]{1,0:T(8,128)(2,1)S(1)}, u32[]{:S(2)}, u32[]{:S(2)}) collective-permute-start(bf16[8,6144]{1,0:T(8,128)(2,1)S(1)} %get-tuple-element.11), channel_id=1, source_target_pairs={{0,4},{1,5},{2,6},{3,7},{4,0},{5,1},{6,2},{7,3},{8,12},{9,13},{10,... | collective-permute-start | bytes 294920 | tf_op jit(solution)/shard_map/ppermute | solution.py:139
  58.0 4.2 %collective-permute-start.9 = (bf16[4,6144]{1,0:T(4,128)(2,1)S(1)}, bf16[4,6144]{1,0:T(4,128)(2,1)S(1)}, u32[]{:S(2)}, u32[]{:S(2)}) collective-permute-start(bf16[4,6144]{1,0:T(4,128)(2,1)S(1)} %slice.36), channel_id=1, source_target_pairs={{0,1},{1,0},{2,3},{3,2},{4,5},{5,4},{6,7},{7,6},{8,9},{9,8},{10,11... | collective-permute-start | bytes 147464 | tf_op jit(solution)/shard_map/ppermute | solution.py:139

commit v3 on v2

--- a/solution.py
+++ b/solution.py
@@ -12,7 +12,8 @@
 LANES = 128
 MIB = 1 << 20
 MIN_ROWS = 128
-SLOTS = 3
+SLOTS = 2
+HELD = 3
 
 VMEM = pl.BlockSpec(memory_space=pltpu.VMEM)
 HBM = pl.BlockSpec(memory_space=pl.ANY)
@@ -26,11 +27,22 @@
     return jnp.sum(jnp.where(first == second, spread, 0.0), axis=1, keepdims=True)
 
 
-def norm_kernel(hidden_ref, gain_ref, routes_ref, gates_ref, payload_ref):
+def norm_kernel(*refs):
+    sources, payload_ref, buffers, sems = refs[:4], refs[4], refs[5:9], refs[9]
+    copies = [
+        pltpu.make_async_copy(source, buffer, sems.at[i])
+        for i, (source, buffer) in enumerate(zip(sources, buffers))
+    ]
+    for copy in copies:
+        copy.start()
+    for copy in copies:
+        copy.wait()
+    hidden_ref, gain_ref, routes_ref, gates_ref = buffers
     rows, width = hidden_ref.shape
     values = hidden_ref[...].astype(jnp.float32)
     inverse = lax.rsqrt(jnp.mean(values * values, axis=-1, keepdims=True) + EPSILON)
-    normed = (values * inverse * gain_ref[...].astype(jnp.float32)).astype(jnp.bfloat16)
+    gain = gain_ref[...].astype(jnp.float32).reshape(1, width)
+    normed = (values * inverse * gain).astype(jnp.bfloat16)
     routes = routes_ref[...].astype(jnp.float32)
     gates = gates_ref[...].astype(jnp.float32)
     labels = lax.broadcasted_iota(jnp.int32, (rows, LANES), 1).astype(jnp.float32)
@@ -62,16 +74,27 @@
     )(*pieces)
 
 
+def fetch_kernel(after_ref, w_down_ref, held_ref, sem):
+    del after_ref
+    columns = held_ref.shape[1]
+    copy = pltpu.make_async_copy(w_down_ref.at[:, pl.ds(0, columns)], held_ref, sem)
+    copy.start()
+    copy.wait()
+
+
 def expert_kernel(
-    devices, own_ref, other_ref, gate_ref, w_up_ref, w_down_ref,
+    devices, even_ref, odd_ref, other_even_ref, other_odd_ref, gate_ref, held_ref, w_up_ref, w_down_ref,
     kept_ref, sent_ref, x, hidden, up_slots, down_slots, sems,
 ):
-    half = own_ref.shape[0]
+    pieces = (even_ref, odd_ref, other_even_ref, other_odd_ref)
+    quarter = even_ref.shape[0]
+    half = 2 * quarter
     rows, width = x.shape
     units = hidden.shape[1]
     up_block, down_block = up_slots.shape[2], down_slots.shape[2]
     ups = units // up_block
-    downs = width // down_block
+    helds = held_ref.shape[1] // down_block
+    downs = width // down_block - helds
     slots = up_slots.shape[0]
 
     def copy(i):
@@ -79,7 +102,7 @@
             source = w_up_ref.at[:, pl.ds(i * up_block, up_block)]
             return pltpu.make_async_copy(source, up_slots.at[i % slots], sems.at[i % slots])
         j = i - ups
-        source = w_down_ref.at[:, pl.ds(j * down_block, down_block)]
+        source = w_down_ref.at[:, pl.ds((helds + j) * down_block, down_block)]
         return pltpu.make_async_copy(source, down_slots.at[j % slots], sems.at[slots + j % slots])
 
     def start(i):
@@ -88,19 +111,19 @@
 
     for i in range(slots):
         start(i)
-    x[:half] = own_ref[:, :width]
-    x[half : 2 * half] = other_ref[:, :width]
+    for i, piece in enumerate(pieces):
+        x[i * quarter : (i + 1) * quarter] = piece[:, :width]
     if rows > 2 * half:
         x[2 * half :] = jnp.zeros((rows - 2 * half, width), x.dtype)
 
     expert = lax.axis_index(("side", "attn")) // (devices // EXPERTS)
-    labels = lax.broadcasted_iota(jnp.int32, (half, LANES), 1)
+    labels = lax.broadcasted_iota(jnp.int32, (quarter, LANES), 1)
 
     def weight_of(ref):
         tail = ref[:, width:].astype(jnp.float32)
         return jnp.sum(jnp.where(labels == expert, tail, 0.0), axis=1, keepdims=True)
 
-    kept_weight, sent_weight = weight_of(own_ref), weight_of(other_ref)
+    weights = [weight_of(piece) for piece in pieces]
 
     inputs = x[...]
     for i in range(ups):
@@ -113,16 +136,21 @@
 
     activations = hidden[...]
 
-    def finish(weights, first, size):
-        out = jnp.dot(activations, weights, preferred_element_type=jnp.float32)
-        columns = pl.ds(first, size)
-        kept_ref[:, columns] = (out[:half] * kept_weight).astype(kept_ref.dtype)
-        sent_ref[:, columns] = (out[half : 2 * half] * sent_weight).astype(sent_ref.dtype)
-
-    for j in range(downs):
-        copy(ups + j).wait()
-        finish(down_slots[j % slots], j * down_block, down_block)
-        start(ups + j + slots)
+    def finish(block, first):
+        out = jnp.dot(activations, block, preferred_element_type=jnp.float32)
+        columns = pl.ds(first, down_block)
+        for i, weight in enumerate(weights):
+            target = (kept_ref, sent_ref)[i // 2]
+            piece = out[i * quarter : (i + 1) * quarter] * weight
+            target[i % 2 * quarter : (i % 2 + 1) * quarter, columns] = piece.astype(target.dtype)
+
+    for j in range(max(helds, downs)):
+        if j < helds:
+            finish(held_ref[:, j * down_block : (j + 1) * down_block], j * down_block)
+        if j < downs:
+            copy(ups + j).wait()
+            finish(down_slots[j % slots], (helds + j) * down_block)
+            start(ups + j + slots)
 
 
 def divisor(size, wanted):
@@ -146,29 +174,48 @@
     devices = lax.axis_size("side") * chips
     half = rows * chips
     dtype = jnp.bfloat16
+    w_up = pltpu.with_memory_space_constraint(w_up, pltpu.HBM)
+    w_down = pltpu.with_memory_space_constraint(w_down, pltpu.HBM)
     small = half <= 32
-    kernel_bytes = (22 if small else 32) * MIB
+    kernel_bytes = (61 if small else 128) * (MIB // 4)
     up_block, down_block = divisor(units, 256), 512
-
+    resident = HELD * down_block
+
+    sources = [hidden_in, norm_gain, routes.T, route_gates.T]
     payload = pl.pallas_call(
         norm_kernel,
-        in_specs=[VMEM] * 4,
+        in_specs=[HBM] * 4,
         out_specs=VMEM,
         out_shape=jax.ShapeDtypeStruct((rows, width + LANES), dtype),
-        compiler_params=pltpu.CompilerParams(vmem_limit_bytes=4*MIB),
+        scratch_shapes=[pltpu.VMEM(source.shape, source.dtype) for source in sources]
+        + [pltpu.SemaphoreType.DMA((4,))],
+        compiler_params=pltpu.CompilerParams(vmem_limit_bytes=4 * MIB),
         cost_estimate=pl.CostEstimate(flops=10**11, bytes_accessed=10**6, transcendentals=0),
         name="norm",
-    )(hidden_in, norm_gain.reshape(1, width), routes.T, route_gates.T)
-
-    pair = join([payload, swap_chips(payload, 1)], 4*MIB)
-    far = [swap_chips(pair, d) for d in range(2, chips, 2)]
-    own = join([pair] + far, 4*MIB)
-    other = swap_sides(own)
+    )(*[pltpu.with_memory_space_constraint(source, pltpu.HBM) for source in sources])
+
+    even = join([payload] + [swap_chips(payload, d) for d in range(2, chips, 2)], 4 * MIB)
+    odd = swap_chips(even, 1)
+    other_even = swap_sides(even)
+    held = pl.pallas_call(
+        fetch_kernel,
+        in_specs=[HBM] * 2,
+        out_specs=VMEM,
+        out_shape=pltpu.VMEM((units, resident), dtype),
+        scratch_shapes=[pltpu.SemaphoreType.DMA],
+        compiler_params=pltpu.CompilerParams(vmem_limit_bytes=4 * MIB),
+        cost_estimate=pl.CostEstimate(
+            flops=0, bytes_accessed=2 * units * resident, transcendentals=0
+        ),
+        name="fetch",
+    )(even, w_down)
+    odd, held = lax.optimization_barrier((odd, held))
+    other_odd = swap_sides(odd)
 
     padded = max(2 * half, MIN_ROWS)
     kept, sent = pl.pallas_call(
         functools.partial(expert_kernel, devices),
-        in_specs=[VMEM] * 3 + [HBM] * 2,
+        in_specs=[VMEM] * 6 + [HBM] * 2,
         out_specs=[VMEM] * 2,
         out_shape=[jax.ShapeDtypeStruct((half, width), dtype)] * 2,
         scratch_shapes=[
@@ -181,14 +228,17 @@
         compiler_params=pltpu.CompilerParams(vmem_limit_bytes=kernel_bytes),
         cost_estimate=pl.CostEstimate(
             flops=12 * half * width * units,
-            bytes_accessed=2 * units * 2 * width,
+            bytes_accessed=2 * units * (2 * width - resident),
             transcendentals=2 * half * units,
         ),
         name="experts",
     )(
-        own,
-        other,
+        even,
+        odd,
+        other_even,
+        other_odd,
         pltpu.with_memory_space_constraint(w_gate, pltpu.VMEM),
+        pltpu.with_memory_space_constraint(held, pltpu.VMEM),
         w_up,
         w_down,
     )
@@ -197,12 +247,12 @@
         return sum(v.astype(jnp.float32) for v in values)
 
     summed = add([kept, swap_sides(sent)]).astype(dtype)
-    step = 2 * rows
+    middle = half // 2
+    plane = add([summed[:middle], swap_chips(summed[middle:], 1)]).astype(dtype)
     arrived = [
-        swap_chips(summed[d // 2 * step : (d // 2 + 1) * step], d) for d in range(2, chips, 2)
+        swap_chips(plane[d // 2 * rows : (d // 2 + 1) * rows], d) for d in range(2, chips, 2)
     ]
-    total = add([summed[:step]] + arrived)
-    return add([total[:rows], swap_chips(total[rows:].astype(dtype), 1)]).astype(dtype)
+    return add([plane[:rows]] + arrived).astype(dtype)
 
 
 def solution(mesh):

time: 63 us -> 64.5 us (1.024)
  Pallas kernels: 22.2 us -> 31.5 us
  waiting for transfers between devices: 23.6 us -> 19 us
  local copies, waits for them, and re-layouts: 2.9 us -> 0.11 us
    pallas_call x1, Pallas kernels: 22 us -> 27 us  [shards(): pl.pallas_call(functools.partial(expert_kernel, devices), in_specs=[VMEM]...]
    ppermute x8, waiting for transfers between devices: 20.3 us -> 15.7 us  [swap_chips(): lax.ppermute(values, 'attn', [(i, i ^ distance) for i in range(chips)])]
    pallas_call x1 -> x2, Pallas kernels: 0.16 us -> 4.39 us  [the longest x1 3.24 us: shards(): pl.pallas_call(fetch_kernel, in_specs=[HBM] * 2, out_specs=VMEM, out_shap...]
    unnamed x8 -> x16, local copies, waits for them, and re-layouts: 2.13 us -> 0.03 us
    reshape x1 -> x0, local copies, waits for them, and re-layouts: 0.72 us -> none  [shards(): norm_gain.reshape(1, width)]
    ppermute x2 -> x3, waiting for transfers between devices: 3.33 us -> 3.25 us  [swap_sides(): lax.ppermute(values, 'side', [(i, sides - 1 - i) for i in range(sides)])]
  transfers between devices with their start and end apart: 10 -> 11, of which waited for: 9 -> 9; matrix products, arithmetic and copies ran while one was open for 0% -> 0% of each run, Pallas kernels for 0% -> 5%
where the time goes in v3:
time: 64.5 us; the launch traced here: 64.2 us
  Pallas kernels  31.5 us (49%)
  waiting for transfers between devices  19 us (29%)
  starting transfers between devices  12.7 us (20%)
  other arithmetic  0.82 us (1%)
    pallas_call x1, Pallas kernels, shards(): pl.pallas_call(functools.partial(expert_kernel, devices), in_specs=[VMEM]...  27 us
    ppermute x8, waiting for transfers between devices, swap_chips(): lax.ppermute(values, 'attn', [(i, i ^ distance) for i in range(chips)])  15.7 us
    ppermute x8, starting transfers between devices, swap_chips(): lax.ppermute(values, 'attn', [(i, i ^ distance) for i in range(chips)])  12.5 us
    ppermute x3, waiting for transfers between devices, swap_sides(): lax.ppermute(values, 'side', [(i, sides - 1 - i) for i in range(sides)])  3.25 us
    pallas_call x1, Pallas kernels, shards(): pl.pallas_call(fetch_kernel, in_specs=[HBM] * 2, out_specs=VMEM, out_shap...  3.24 us
  transfers between devices with their start and end apart: 11, of which 9 were waited for; matrix products, arithmetic and copies ran while one was open for 0% of the time, Pallas kernels for 5%

profile of v3, /device:TPU:0, one launch (start us, length us, event | category | flops | bytes accessed | tf_op | source)
XLA Modules:
  0.0 64.2 jit_solution(11501205513698244481)
XLA Ops:
  0.0 0.0 slice-start
  0.0 0.0 slice-start.1
  0.0 0.0 slice-start.2
  0.0 0.0 slice-start.3
  0.0 0.0 slice-start.4
  0.0 0.0 slice-start.5
  0.0 0.0 slice-start.6
  0.0 0.0 slice-start.7
  0.0 1.1 %norm.1.refs_0_ = bf16[4,6272]{1,0:T(4,128)(2,1)S(1)} custom-call(bf16[4,6144]{1,0:T(4,128)(2,1)} %refs_0_.1, bf16[6144]{0:T(1024)(128)(2,1)} %refs_1_.1, s32[2,4]{1,0:T(2,128)} %bitcast.4, bf16[2,4]{1,0:T(2,128)(2,1)} %bitcast.5), custom_call_target="tpu_custom_call" | custom-call | flops 99999997952 | bytes 1000000 | tf_op jit(solution)/shard_map/norm/pallas_call | solution.py:185
  1.2 5.1 %collective-permute-start.2 = (bf16[4,6272]{1,0:T(4,128)(2,1)S(1)}, bf16[4,6272]{1,0:T(4,128)(2,1)S(1)}, u32[]{:S(2)}, u32[]{:S(2)}) collective-permute-start(bf16[4,6272]{1,0:T(4,128)(2,1)S(1)} %norm.1.refs_0_), channel_id=1, source_target_pairs={{0,6},{1,7},{2,4},{3,5},{4,2},{5,3},{6,0},{7,1},{8,14},{9,15},{10,... | collective-permute-start | bytes 150536 | tf_op jit(solution)/shard_map/ppermute | solution.py:167
  6.3 0.0 collective-permute-start.1
  6.3 0.6 collective-permute-start
  7.0 1.6 %collective-permute-done.2.refs_3_ = bf16[4,6272]{1,0:T(4,128)(2,1)S(1)} collective-permute-done((bf16[4,6272]{1,0:T(4,128)(2,1)S(1)}, bf16[4,6272]{1,0:T(4,128)(2,1)S(1)}, u32[]{:S(2)}, u32[]{:S(2)}) %collective-permute-start.2) | collective-permute-done | bytes 50208 | tf_op jit(solution)/shard_map/ppermute | solution.py:167
  8.6 2.7 %collective-permute-done.1.refs_2_ = bf16[4,6272]{1,0:T(4,128)(2,1)S(1)} collective-permute-done((bf16[4,6272]{1,0:T(4,128)(2,1)S(1)}, bf16[4,6272]{1,0:T(4,128)(2,1)S(1)}, u32[]{:S(2)}, u32[]{:S(2)}) %collective-permute-start.1) | collective-permute-done | bytes 50208 | tf_op jit(solution)/shard_map/ppermute | solution.py:167
  11.3 0.0 collective-permute-done.refs_1_
  11.3 0.1 join.1.after_ref.even_ref
  11.4 1.6 %collective-permute-start.3 = (bf16[16,6272]{1,0:T(8,128)(2,1)S(1)}, bf16[16,6272]{1,0:T(8,128)(2,1)S(1)}, u32[]{:S(2)}, u32[]{:S(2)}) collective-permute-start(bf16[16,6272]{1,0:T(8,128)(2,1)S(1)} %join.1.after_ref.even_ref), channel_id=1, source_target_pairs={{0,1},{1,0},{2,3},{3,2},{4,5},{5,4},{6,7},{7,6},{8,9},{9,8},{10,11... | collective-permute-start | bytes 602120 | tf_op jit(solution)/shard_map/ppermute | solution.py:167
  13.0 0.0 collective-permute-start.4
  13.0 3.2 %fetch.1.held_ref = bf16[2560,1536]{1,0:T(8,128)(2,1)S(1)} custom-call(bf16[16,6272]{1,0:T(8,128)(2,1)S(1)} %join.1.after_ref.even_ref, bf16[2560,6144]{1,0:T(8,128)(2,1)} %w_down_ref.3), custom_call_target="tpu_custom_call" | custom-call | bytes 7864320 | tf_op jit(solution)/shard_map/fetch/pallas_call | solution.py:200
  16.2 1.1 %collective-permute-done.3.odd_ref = bf16[16,6272]{1,0:T(8,128)(2,1)S(1)} collective-permute-done((bf16[16,6272]{1,0:T(8,128)(2,1)S(1)}, bf16[16,6272]{1,0:T(8,128)(2,1)S(1)}, u32[]{:S(2)}, u32[]{:S(2)}) %collective-permute-start.3) | collective-permute-done | bytes 200736 | tf_op jit(solution)/shard_map/ppermute | solution.py:167
  17.3 0.0 collective-permute-start.5
  17.3 0.0 collective-permute-done.4.other_even_ref
  17.3 1.4 %collective-permute-done.5.other_odd_ref = bf16[16,6272]{1,0:T(8,128)(2,1)S(1)} collective-permute-done((bf16[16,6272]{1,0:T(8,128)(2,1)S(1)}, bf16[16,6272]{1,0:T(8,128)(2,1)S(1)}, u32[]{:S(2)}, u32[]{:S(2)}) %collective-permute-start.5) | collective-permute-done | bytes 200736 | tf_op jit(solution)/shard_map/ppermute | solution.py:162
  18.8 0.0 slice-done
  18.8 0.0 slice-done.1
  18.8 0.0 slice-done.2
  18.8 0.0 slice-done.3
  18.8 0.0 slice-done.4
  18.8 0.0 slice-done.5
  18.8 0.0 slice-done.6
  18.8 0.0 slice-done.7
  18.8 27.0 %experts.1 = (bf16[32,6144]{1,0:T(8,128)(2,1)S(1)}, bf16[32,6144]{1,0:T(8,128)(2,1)}) custom-call(bf16[16,6272]{1,0:T(8,128)(2,1)S(1)} %join.1.after_ref.even_ref, bf16[16,6272]{1,0:T(8,128)(2,1)S(1)} %collective-permute-done.3.odd_ref, bf16[16,6272]{1,0:T(8,128)(2,1)S(1)} %collective-permute-done.4.other_even_ref, ...), custom_call_target="tpu_custom_call" | custom-call | flops 6039797760 | bytes 55050240 | tf_op jit(solution)/shard_map/experts/pallas_call | solution.py:216
  45.8 0.2 collective-permute-start.6
  46.0 1.8 %collective-permute-done.6 = bf16[32,6144]{1,0:T(8,128)(2,1)S(1)} collective-permute-done((bf16[32,6144]{1,0:T(8,128)(2,1)}, bf16[32,6144]{1,0:T(8,128)(2,1)S(1)}, u32[]{:S(2)}, u32[]{:S(2)}) %collective-permute-start.6) | collective-permute-done | bytes 393248 | tf_op jit(solution)/shard_map/ppermute | solution.py:162
  47.8 0.1 add_convert_fusion
  48.0 1.6 %collective-permute-start.7 = (bf16[16,6144]{1,0:T(8,128)(2,1)S(1)}, bf16[16,6144]{1,0:T(8,128)(2,1)S(1)}, u32[]{:S(2)}, u32[]{:S(2)}) collective-permute-start(bf16[16,6144]{1,0:T(8,128)(2,1)S(1)} %slice.25), channel_id=1, source_target_pairs={{0,1},{1,0},{2,3},{3,2},{4,5},{5,4},{6,7},{7,6},{8,9},{9,8},{10,11... | collective-permute-start | bytes 589832 | tf_op jit(solution)/shard_map/ppermute | solution.py:167
  49.6 5.4 %collective-permute-done.7 = bf16[16,6144]{1,0:T(8,128)(2,1)S(1)} collective-permute-done((bf16[16,6144]{1,0:T(8,128)(2,1)S(1)}, bf16[16,6144]{1,0:T(8,128)(2,1)S(1)}, u32[]{:S(2)}, u32[]{:S(2)}) %collective-permute-start.7) | collective-permute-done | bytes 196640 | tf_op jit(solution)/shard_map/ppermute | solution.py:167
  55.0 0.1 fusion
  55.1 0.8 %collective-permute-start.8 = (bf16[4,6144]{1,0:T(4,128)(2,1)S(1)}, bf16[4,6144]{1,0:T(4,128)(2,1)S(1)}, u32[]{:S(2)}, u32[]{:S(2)}) collective-permute-start(bf16[4,6144]{1,0:T(4,128)(2,1)S(1)} %get-tuple-element.13), channel_id=1, source_target_pairs={{0,2},{1,3},{2,0},{3,1},{4,6},{5,7},{6,4},{7,5},{8,10},{9,11},{10,... | collective-permute-start | bytes 147464 | tf_op jit(solution)/shard_map/ppermute | solution.py:167
  55.9 2.6 %collective-permute-start.10 = (bf16[4,6144]{1,0:T(4,128)(2,1)S(1)}, bf16[4,6144]{1,0:T(4,128)(2,1)S(1)}, u32[]{:S(2)}, u32[]{:S(2)}) collective-permute-start(bf16[4,6144]{1,0:T(4,128)(2,1)S(1)} %get-tuple-element.14), channel_id=1, source_target_pairs={{0,6},{1,7},{2,4},{3,5},{4,2},{5,3},{6,0},{7,1},{8,14},{9,15},{10,... | collective-permute-start | bytes 147464 | tf_op jit(solution)/shard_map/ppermute | solution.py:167
  58.5 0.1 collective-permute-start.9
  58.6 0.6 collective-permute-done.8
  59.3 2.6 %collective-permute-done.10 = bf16[4,6144]{1,0:T(4,128)(2,1)S(1)} collective-permute-done((bf16[4,6144]{1,0:T(4,128)(2,1)S(1)}, bf16[4,6144]{1,0:T(4,128)(2,1)S(1)}, u32[]{:S(2)}, u32[]{:S(2)}) %collective-permute-start.10) | collective-permute-done | bytes 49184 | tf_op jit(solution)/shard_map/ppermute | solution.py:167
  61.9 1.6 %collective-permute-done.9 = bf16[4,6144]{1,0:T(4,128)(2,1)S(1)} collective-permute-done((bf16[4,6144]{1,0:T(4,128)(2,1)S(1)}, bf16[4,6144]{1,0:T(4,128)(2,1)S(1)}, u32[]{:S(2)}, u32[]{:S(2)}) %collective-permute-start.9) | collective-permute-done | bytes 49184 | tf_op jit(solution)/shard_map/ppermute | solution.py:167
  63.5 0.7 %add_convert_fusion.2 = bf16[4,6144]{1,0:T(4,128)(2,1)} fusion(bf16[4,6144]{1,0:T(4,128)(2,1)S(1)} %collective-permute-done.10, bf16[4,6144]{1,0:T(4,128)(2,1)S(1)} %collective-permute-done.9, bf16[4,6144]{1,0:T(4,128)(2,1)S(1)} %collective-permute-done.8, bf16[16,6144]{1,0:T(8,128)(2,1)S(1)} %add_convert_fusion.1), kind=kLoop, calls=%fused_computation.2 | loop fusion | flops 196608 | bytes 245760 | tf_op jit(solution)/shard_map/convert_element_type | solution.py:255
  (3 shorter events, 0.1 us)
Async XLA Ops:
  0.0 18.8 %slice-start = ((s8[31457280]{0:T(1024)(128)(4,1)}), s8[4194304]{0:T(1024)(128)(4,1)S(1)}, s32[]{:S(2)}) async-start(s8[31457280]{0:T(1024)(128)(4,1)} %bitcast.2), calls=%async_computation | async-start | bytes 8388608
  0.0 18.8 %slice-start.1 = ((s8[31457280]{0:T(1024)(128)(4,1)}), s8[4194304]{0:T(1024)(128)(4,1)S(1)}, s32[]{:S(2)}) async-start(s8[31457280]{0:T(1024)(128)(4,1)} %bitcast.2), calls=%async_computation.1 | async-start | bytes 8388608
  0.0 18.8 %slice-start.2 = ((s8[31457280]{0:T(1024)(128)(4,1)}), s8[4194304]{0:T(1024)(128)(4,1)S(1)}, s32[]{:S(2)}) async-start(s8[31457280]{0:T(1024)(128)(4,1)} %bitcast.2), calls=%async_computation.2 | async-start | bytes 8388608
  0.0 18.8 %slice-start.3 = ((s8[31457280]{0:T(1024)(128)(4,1)}), s8[4194304]{0:T(1024)(128)(4,1)S(1)}, s32[]{:S(2)}) async-start(s8[31457280]{0:T(1024)(128)(4,1)} %bitcast.2), calls=%async_computation.3 | async-start | bytes 8388608
  0.0 18.8 %slice-start.4 = ((s8[31457280]{0:T(1024)(128)(4,1)}), s8[4194304]{0:T(1024)(128)(4,1)S(1)}, s32[]{:S(2)}) async-start(s8[31457280]{0:T(1024)(128)(4,1)} %bitcast.2), calls=%async_computation.4 | async-start | bytes 8388608
  0.0 18.8 %slice-start.5 = ((s8[31457280]{0:T(1024)(128)(4,1)}), s8[4194304]{0:T(1024)(128)(4,1)S(1)}, s32[]{:S(2)}) async-start(s8[31457280]{0:T(1024)(128)(4,1)} %bitcast.2), calls=%async_computation.5 | async-start | bytes 8388608
  0.0 18.8 %slice-start.6 = ((s8[31457280]{0:T(1024)(128)(4,1)}), s8[4194304]{0:T(1024)(128)(4,1)S(1)}, s32[]{:S(2)}) async-start(s8[31457280]{0:T(1024)(128)(4,1)} %bitcast.2), calls=%async_computation.6 | async-start | bytes 8388608
  0.0 18.8 %slice-start.7 = ((s8[31457280]{0:T(1024)(128)(4,1)}), s8[2097152]{0:T(1024)(128)(4,1)S(1)}, s32[]{:S(2)}) async-start(s8[31457280]{0:T(1024)(128)(4,1)} %bitcast.2), calls=%async_computation.7 | async-start | bytes 4194304
  1.2 7.4 %collective-permute-start.2 = (bf16[4,6272]{1,0:T(4,128)(2,1)S(1)}, bf16[4,6272]{1,0:T(4,128)(2,1)S(1)}, u32[]{:S(2)}, u32[]{:S(2)}) collective-permute-start(bf16[4,6272]{1,0:T(4,128)(2,1)S(1)} %norm.1.refs_0_), channel_id=1, source_target_pairs={{0,6},{1,7},{2,4},{3,5},{4,2},{5,3},{6,0},{7,1},{8,14},{9,15},{10,... | collective-permute-start | bytes 150536 | tf_op jit(solution)/shard_map/ppermute | solution.py:167
  6.3 5.0 %collective-permute-start.1 = (bf16[4,6272]{1,0:T(4,128)(2,1)S(1)}, bf16[4,6272]{1,0:T(4,128)(2,1)S(1)}, u32[]{:S(2)}, u32[]{:S(2)}) collective-permute-start(bf16[4,6272]{1,0:T(4,128)(2,1)S(1)} %norm.1.refs_0_), channel_id=1, source_target_pairs={{0,4},{1,5},{2,6},{3,7},{4,0},{5,1},{6,2},{7,3},{8,12},{9,13},{10,... | collective-permute-start | bytes 150536 | tf_op jit(solution)/shard_map/ppermute | solution.py:167
  6.3 5.0 %collective-permute-start = (bf16[4,6272]{1,0:T(4,128)(2,1)S(1)}, bf16[4,6272]{1,0:T(4,128)(2,1)S(1)}, u32[]{:S(2)}, u32[]{:S(2)}) collective-permute-start(bf16[4,6272]{1,0:T(4,128)(2,1)S(1)} %norm.1.refs_0_), channel_id=1, source_target_pairs={{0,2},{1,3},{2,0},{3,1},{4,6},{5,7},{6,4},{7,5},{8,10},{9,11},{10,... | collective-permute-start | bytes 150536 | tf_op jit(solution)/shard_map/ppermute | solution.py:167
  11.4 5.9 %collective-permute-start.3 = (bf16[16,6272]{1,0:T(8,128)(2,1)S(1)}, bf16[16,6272]{1,0:T(8,128)(2,1)S(1)}, u32[]{:S(2)}, u32[]{:S(2)}) collective-permute-start(bf16[16,6272]{1,0:T(8,128)(2,1)S(1)} %join.1.after_ref.even_ref), channel_id=1, source_target_pairs={{0,1},{1,0},{2,3},{3,2},{4,5},{5,4},{6,7},{7,6},{8,9},{9,8},{10,11... | collective-permute-start | bytes 602120 | tf_op jit(solution)/shard_map/ppermute | solution.py:167
  13.0 4.3 %collective-permute-start.4 = (bf16[16,6272]{1,0:T(8,128)(2,1)S(1)}, bf16[16,6272]{1,0:T(8,128)(2,1)S(1)}, u32[]{:S(2)}, u32[]{:S(2)}) collective-permute-start(bf16[16,6272]{1,0:T(8,128)(2,1)S(1)} %join.1.after_ref.even_ref), channel_id=1, source_target_pairs={{0,8},{8,0},{1,9},{9,1},{2,10},{10,2},{3,11},{11,3},{4,12},{12,4},... | collective-permute-start | bytes 602120 | tf_op jit(solution)/shard_map/ppermute | solution.py:162
  17.3 1.4 %collective-permute-start.5 = (bf16[16,6272]{1,0:T(8,128)(2,1)S(1)}, bf16[16,6272]{1,0:T(8,128)(2,1)S(1)}, u32[]{:S(2)}, u32[]{:S(2)}) collective-permute-start(bf16[16,6272]{1,0:T(8,128)(2,1)S(1)} %collective-permute-done.3.odd_ref), channel_id=1, source_target_pairs={{0,8},{8,0},{1,9},{9,1},{2,10},{10,2},{3,11},{11,3},{4,12},{12,4},... | collective-permute-start | bytes 602120 | tf_op jit(solution)/shard_map/ppermute | solution.py:162
  45.8 2.0 %collective-permute-start.6 = (bf16[32,6144]{1,0:T(8,128)(2,1)}, bf16[32,6144]{1,0:T(8,128)(2,1)S(1)}, u32[]{:S(2)}, u32[]{:S(2)}) collective-permute-start(bf16[32,6144]{1,0:T(8,128)(2,1)} %get-tuple-element.12), channel_id=1, source_target_pairs={{0,8},{8,0},{1,9},{9,1},{2,10},{10,2},{3,11},{11,3},{4,12},{12,4},... | collective-permute-start | bytes 1179656 | tf_op jit(solution)/shard_map/ppermute | solution.py:162
  48.0 7.0 %collective-permute-start.7 = (bf16[16,6144]{1,0:T(8,128)(2,1)S(1)}, bf16[16,6144]{1,0:T(8,128)(2,1)S(1)}, u32[]{:S(2)}, u32[]{:S(2)}) collective-permute-start(bf16[16,6144]{1,0:T(8,128)(2,1)S(1)} %slice.25), channel_id=1, source_target_pairs={{0,1},{1,0},{2,3},{3,2},{4,5},{5,4},{6,7},{7,6},{8,9},{9,8},{10,11... | collective-permute-start | bytes 589832 | tf_op jit(solution)/shard_map/ppermute | solution.py:167
  55.1 4.2 %collective-permute-start.8 = (bf16[4,6144]{1,0:T(4,128)(2,1)S(1)}, bf16[4,6144]{1,0:T(4,128)(2,1)S(1)}, u32[]{:S(2)}, u32[]{:S(2)}) collective-permute-start(bf16[4,6144]{1,0:T(4,128)(2,1)S(1)} %get-tuple-element.13), channel_id=1, source_target_pairs={{0,2},{1,3},{2,0},{3,1},{4,6},{5,7},{6,4},{7,5},{8,10},{9,11},{10,... | collective-permute-start | bytes 147464 | tf_op jit(solution)/shard_map/ppermute | solution.py:167
  55.9 6.0 %collective-permute-start.10 = (bf16[4,6144]{1,0:T(4,128)(2,1)S(1)}, bf16[4,6144]{1,0:T(4,128)(2,1)S(1)}, u32[]{:S(2)}, u32[]{:S(2)}) collective-permute-start(bf16[4,6144]{1,0:T(4,128)(2,1)S(1)} %get-tuple-element.14), channel_id=1, source_target_pairs={{0,6},{1,7},{2,4},{3,5},{4,2},{5,3},{6,0},{7,1},{8,14},{9,15},{10,... | collective-permute-start | bytes 147464 | tf_op jit(solution)/shard_map/ppermute | solution.py:167
  58.5 5.0 %collective-permute-start.9 = (bf16[4,6144]{1,0:T(4,128)(2,1)S(1)}, bf16[4,6144]{1,0:T(4,128)(2,1)S(1)}, u32[]{:S(2)}, u32[]{:S(2)}) collective-permute-start(bf16[4,6144]{1,0:T(4,128)(2,1)S(1)} %get-tuple-element.15), channel_id=1, source_target_pairs={{0,4},{1,5},{2,6},{3,7},{4,0},{5,1},{6,2},{7,3},{8,12},{9,13},{10,... | collective-permute-start | bytes 147464 | tf_op jit(solution)/shard_map/ppermute | solution.py:167

commit v4 on v3

--- a/solution.py
+++ b/solution.py
@@ -12,8 +12,8 @@
 LANES = 128
 MIB = 1 << 20
 MIN_ROWS = 128
-SLOTS = 2
-HELD = 3
+SLOTS = 4
+HELD = 2
 
 VMEM = pl.BlockSpec(memory_space=pltpu.VMEM)
 HBM = pl.BlockSpec(memory_space=pl.ANY)
@@ -83,33 +83,38 @@
 
 
 def expert_kernel(
-    devices, even_ref, odd_ref, other_even_ref, other_odd_ref, gate_ref, held_ref, w_up_ref, w_down_ref,
-    kept_ref, sent_ref, x, hidden, up_slots, down_slots, sems,
+    devices, up_block, down_block, even_ref, odd_ref, other_even_ref, other_odd_ref, gate_ref, held_ref,
+    w_up_ref, w_down_ref, kept_ref, sent_ref, x, hidden, slots, sems,
 ):
     pieces = (even_ref, odd_ref, other_even_ref, other_odd_ref)
     quarter = even_ref.shape[0]
     half = 2 * quarter
     rows, width = x.shape
     units = hidden.shape[1]
-    up_block, down_block = up_slots.shape[2], down_slots.shape[2]
-    ups = units // up_block
+    count = slots.shape[0]
+    depth = width // 2
+    ups = 2 * units // up_block
     helds = held_ref.shape[1] // down_block
     downs = width // down_block - helds
-    slots = up_slots.shape[0]
+
+    def slot(i):
+        if i < ups:
+            return slots.at[i % count, pl.ds(0, depth), pl.ds(0, up_block)]
+        return slots.at[i % count, pl.ds(0, units), pl.ds(0, down_block)]
 
     def copy(i):
         if i < ups:
-            source = w_up_ref.at[:, pl.ds(i * up_block, up_block)]
-            return pltpu.make_async_copy(source, up_slots.at[i % slots], sems.at[i % slots])
-        j = i - ups
-        source = w_down_ref.at[:, pl.ds((helds + j) * down_block, down_block)]
-        return pltpu.make_async_copy(source, down_slots.at[j % slots], sems.at[slots + j % slots])
+            lanes = pl.ds(i // 2 * up_block, up_block)
+            source = w_up_ref.at[pl.ds(i % 2 * depth, depth), lanes]
+        else:
+            source = w_down_ref.at[:, pl.ds((helds + i - ups) * down_block, down_block)]
+        return pltpu.make_async_copy(source, slot(i), sems.at[i % count])
 
     def start(i):
         if i < ups + downs:
             copy(i).start()
 
-    for i in range(slots):
+    for i in range(count):
         start(i)
     for i, piece in enumerate(pieces):
         x[i * quarter : (i + 1) * quarter] = piece[:, :width]
@@ -126,12 +131,16 @@
     weights = [weight_of(piece) for piece in pieces]
 
     inputs = x[...]
-    for i in range(ups):
+    for i in range(ups // 2):
         columns = pl.ds(i * up_block, up_block)
         gate = jnp.dot(inputs, gate_ref[:, columns], preferred_element_type=jnp.float32)
-        copy(i).wait()
-        up = jnp.dot(inputs, up_slots[i % slots], preferred_element_type=jnp.float32)
-        start(i + slots)
+        terms = []
+        for k in range(2):
+            copy(2 * i + k).wait()
+            part = inputs[:, k * depth : (k + 1) * depth]
+            terms.append(jnp.dot(part, slot(2 * i + k)[...], preferred_element_type=jnp.float32))
+            start(2 * i + k + count)
+        up = terms[0] + terms[1]
         hidden[:, columns] = (gate / (1.0 + jnp.exp(-gate)) * up).astype(hidden.dtype)
 
     activations = hidden[...]
@@ -149,8 +158,8 @@
             finish(held_ref[:, j * down_block : (j + 1) * down_block], j * down_block)
         if j < downs:
             copy(ups + j).wait()
-            finish(down_slots[j % slots], (helds + j) * down_block)
-            start(ups + j + slots)
+            finish(slot(ups + j)[...], (helds + j) * down_block)
+            start(ups + j + count)
 
 
 def divisor(size, wanted):
@@ -177,8 +186,8 @@
     w_up = pltpu.with_memory_space_constraint(w_up, pltpu.HBM)
     w_down = pltpu.with_memory_space_constraint(w_down, pltpu.HBM)
     small = half <= 32
-    kernel_bytes = (61 if small else 128) * (MIB // 4)
-    up_block, down_block = divisor(units, 256), 512
+    kernel_bytes = (68 if small else 128) * (MIB // 4)
+    up_block, down_block = divisor(units, 512), 512 if units % 512 == 0 else 256
     resident = HELD * down_block
 
     sources = [hidden_in, norm_gain, routes.T, route_gates.T]
@@ -214,16 +223,15 @@
 
     padded = max(2 * half, MIN_ROWS)
     kept, sent = pl.pallas_call(
-        functools.partial(expert_kernel, devices),
+        functools.partial(expert_kernel, devices, up_block, down_block),
         in_specs=[VMEM] * 6 + [HBM] * 2,
         out_specs=[VMEM] * 2,
         out_shape=[jax.ShapeDtypeStruct((half, width), dtype)] * 2,
         scratch_shapes=[
             pltpu.VMEM((padded, width), dtype),
             pltpu.VMEM((padded, units), dtype),
-            pltpu.VMEM((SLOTS, width, up_block), dtype),
-            pltpu.VMEM((SLOTS, units, down_block), dtype),
-            pltpu.SemaphoreType.DMA((2 * SLOTS,)),
+            pltpu.VMEM((SLOTS, max(width // 2, units), max(up_block, down_block)), dtype),
+            pltpu.SemaphoreType.DMA((SLOTS,)),
         ],
         compiler_params=pltpu.CompilerParams(vmem_limit_bytes=kernel_bytes),
         cost_estimate=pl.CostEstimate(

time: 64.5 us -> 57 us (0.88)
  Pallas kernels: 31.5 us -> 23.7 us
    pallas_call x1, Pallas kernels: 27 us -> 19.9 us  [shards(): pl.pallas_call(functools.partial(expert_kernel, devices, up_block, down_b...]
    pallas_call x1, Pallas kernels: 3.24 us -> 2.58 us  [shards(): pl.pallas_call(fetch_kernel, in_specs=[HBM] * 2, out_specs=VMEM, out_shap...]
where the time goes in v4:
time: 57 us; the launch traced here: 56.8 us
  Pallas kernels  23.7 us (42%)
  waiting for transfers between devices  19.4 us (34%)
  starting transfers between devices  12.7 us (22%)
  other arithmetic  0.82 us (1%)
    pallas_call x1, Pallas kernels, shards(): pl.pallas_call(functools.partial(expert_kernel, devices, up_block, down_b...  19.9 us
    ppermute x8, waiting for transfers between devices, swap_chips(): lax.ppermute(values, 'attn', [(i, i ^ distance) for i in range(chips)])  16.4 us
    ppermute x8, starting transfers between devices, swap_chips(): lax.ppermute(values, 'attn', [(i, i ^ distance) for i in range(chips)])  12.5 us
    ppermute x3, waiting for transfers between devices, swap_sides(): lax.ppermute(values, 'side', [(i, sides - 1 - i) for i in range(sides)])  3.04 us
    pallas_call x1, Pallas kernels, shards(): pl.pallas_call(fetch_kernel, in_specs=[HBM] * 2, out_specs=VMEM, out_shap...  2.58 us
    pallas_call x1, Pallas kernels, shards(): pl.pallas_call(norm_kernel, in_specs=[HBM] * 4, out_specs=VMEM, out_shape...  1.15 us
  transfers between devices with their start and end apart: 11, of which 9 were waited for; matrix products, arithmetic and copies ran while one was open for 0% of the time, Pallas kernels for 5%

profile of v4, /device:TPU:0, one launch (start us, length us, event | category | flops | bytes accessed | tf_op | source)
XLA Modules:
  0.0 56.8 jit_solution(2706216337750179692)
XLA Ops:
  0.0 0.0 slice-start
  0.0 0.0 slice-start.1
  0.0 0.0 slice-start.2
  0.0 0.0 slice-start.3
  0.0 0.0 slice-start.4
  0.0 0.0 slice-start.5
  0.0 0.0 slice-start.6
  0.0 0.0 slice-start.7
  0.0 1.1 %norm.1.refs_0_ = bf16[4,6272]{1,0:T(4,128)(2,1)S(1)} custom-call(bf16[4,6144]{1,0:T(4,128)(2,1)} %refs_0_.1, bf16[6144]{0:T(1024)(128)(2,1)} %refs_1_.1, s32[2,4]{1,0:T(2,128)} %bitcast.4, bf16[2,4]{1,0:T(2,128)(2,1)} %bitcast.5), custom_call_target="tpu_custom_call" | custom-call | flops 99999997952 | bytes 1000000 | tf_op jit(solution)/shard_map/norm/pallas_call | solution.py:194
  1.2 5.1 %collective-permute-start.2 = (bf16[4,6272]{1,0:T(4,128)(2,1)S(1)}, bf16[4,6272]{1,0:T(4,128)(2,1)S(1)}, u32[]{:S(2)}, u32[]{:S(2)}) collective-permute-start(bf16[4,6272]{1,0:T(4,128)(2,1)S(1)} %norm.1.refs_0_), channel_id=1, source_target_pairs={{0,6},{1,7},{2,4},{3,5},{4,2},{5,3},{6,0},{7,1},{8,14},{9,15},{10,... | collective-permute-start | bytes 150536 | tf_op jit(solution)/shard_map/ppermute | solution.py:176
  6.3 0.0 collective-permute-start.1
  6.3 0.6 %collective-permute-start = (bf16[4,6272]{1,0:T(4,128)(2,1)S(1)}, bf16[4,6272]{1,0:T(4,128)(2,1)S(1)}, u32[]{:S(2)}, u32[]{:S(2)}) collective-permute-start(bf16[4,6272]{1,0:T(4,128)(2,1)S(1)} %norm.1.refs_0_), channel_id=1, source_target_pairs={{0,2},{1,3},{2,0},{3,1},{4,6},{5,7},{6,4},{7,5},{8,10},{9,11},{10,... | collective-permute-start | bytes 150536 | tf_op jit(solution)/shard_map/ppermute | solution.py:176
  7.0 1.6 %collective-permute-done.2.refs_3_ = bf16[4,6272]{1,0:T(4,128)(2,1)S(1)} collective-permute-done((bf16[4,6272]{1,0:T(4,128)(2,1)S(1)}, bf16[4,6272]{1,0:T(4,128)(2,1)S(1)}, u32[]{:S(2)}, u32[]{:S(2)}) %collective-permute-start.2) | collective-permute-done | bytes 50208 | tf_op jit(solution)/shard_map/ppermute | solution.py:176
  8.6 2.7 %collective-permute-done.1.refs_2_ = bf16[4,6272]{1,0:T(4,128)(2,1)S(1)} collective-permute-done((bf16[4,6272]{1,0:T(4,128)(2,1)S(1)}, bf16[4,6272]{1,0:T(4,128)(2,1)S(1)}, u32[]{:S(2)}, u32[]{:S(2)}) %collective-permute-start.1) | collective-permute-done | bytes 50208 | tf_op jit(solution)/shard_map/ppermute | solution.py:176
  11.3 0.0 collective-permute-done.refs_1_
  11.3 0.1 join.1.after_ref.even_ref
  11.4 1.6 %collective-permute-start.3 = (bf16[16,6272]{1,0:T(8,128)(2,1)S(1)}, bf16[16,6272]{1,0:T(8,128)(2,1)S(1)}, u32[]{:S(2)}, u32[]{:S(2)}) collective-permute-start(bf16[16,6272]{1,0:T(8,128)(2,1)S(1)} %join.1.after_ref.even_ref), channel_id=1, source_target_pairs={{0,1},{1,0},{2,3},{3,2},{4,5},{5,4},{6,7},{7,6},{8,9},{9,8},{10,11... | collective-permute-start | bytes 602120 | tf_op jit(solution)/shard_map/ppermute | solution.py:176
  13.0 0.0 collective-permute-start.4
  13.0 2.6 %fetch.1.held_ref = bf16[2560,1024]{1,0:T(8,128)(2,1)S(1)} custom-call(bf16[16,6272]{1,0:T(8,128)(2,1)S(1)} %join.1.after_ref.even_ref, bf16[2560,6144]{1,0:T(8,128)(2,1)} %w_down_ref.3), custom_call_target="tpu_custom_call" | custom-call | bytes 5242880 | tf_op jit(solution)/shard_map/fetch/pallas_call | solution.py:209
  15.6 1.7 %collective-permute-done.3.odd_ref = bf16[16,6272]{1,0:T(8,128)(2,1)S(1)} collective-permute-done((bf16[16,6272]{1,0:T(8,128)(2,1)S(1)}, bf16[16,6272]{1,0:T(8,128)(2,1)S(1)}, u32[]{:S(2)}, u32[]{:S(2)}) %collective-permute-start.3) | collective-permute-done | bytes 200736 | tf_op jit(solution)/shard_map/ppermute | solution.py:176
  17.3 0.0 collective-permute-start.5
  17.3 0.0 collective-permute-done.4.other_even_ref
  17.3 1.4 %collective-permute-done.5.other_odd_ref = bf16[16,6272]{1,0:T(8,128)(2,1)S(1)} collective-permute-done((bf16[16,6272]{1,0:T(8,128)(2,1)S(1)}, bf16[16,6272]{1,0:T(8,128)(2,1)S(1)}, u32[]{:S(2)}, u32[]{:S(2)}) %collective-permute-start.5) | collective-permute-done | bytes 200736 | tf_op jit(solution)/shard_map/ppermute | solution.py:171
  18.8 0.0 slice-done
  18.8 0.0 slice-done.1
  18.8 0.0 slice-done.2
  18.8 0.0 slice-done.3
  18.8 0.0 slice-done.4
  18.8 0.0 slice-done.5
  18.8 0.0 slice-done.6
  18.8 0.0 slice-done.7
  18.8 19.9 %experts.1 = (bf16[32,6144]{1,0:T(8,128)(2,1)S(1)}, bf16[32,6144]{1,0:T(8,128)(2,1)S(1)}) custom-call(bf16[16,6272]{1,0:T(8,128)(2,1)S(1)} %join.1.after_ref.even_ref, bf16[16,6272]{1,0:T(8,128)(2,1)S(1)} %collective-permute-done.3.odd_ref, bf16[16,6272]{1,0:T(8,128)(2,1)S(1)} %collective-permute-done.4.other_even_ref, ...), custom_call_target="tpu_custom_call" | custom-call | flops 6039797760 | bytes 57671680 | tf_op jit(solution)/shard_map/experts/pallas_call | solution.py:225
  38.7 0.2 collective-permute-start.6
  38.9 1.6 %collective-permute-done.6 = bf16[32,6144]{1,0:T(8,128)(2,1)S(1)} collective-permute-done((bf16[32,6144]{1,0:T(8,128)(2,1)S(1)}, bf16[32,6144]{1,0:T(8,128)(2,1)S(1)}, u32[]{:S(2)}, u32[]{:S(2)}) %collective-permute-start.6) | collective-permute-done | bytes 393248 | tf_op jit(solution)/shard_map/ppermute | solution.py:171
  40.5 0.1 add_convert_fusion
  40.6 1.6 %collective-permute-start.7 = (bf16[16,6144]{1,0:T(8,128)(2,1)S(1)}, bf16[16,6144]{1,0:T(8,128)(2,1)S(1)}, u32[]{:S(2)}, u32[]{:S(2)}) collective-permute-start(bf16[16,6144]{1,0:T(8,128)(2,1)S(1)} %slice.25), channel_id=1, source_target_pairs={{0,1},{1,0},{2,3},{3,2},{4,5},{5,4},{6,7},{7,6},{8,9},{9,8},{10,11... | collective-permute-start | bytes 589832 | tf_op jit(solution)/shard_map/ppermute | solution.py:176
  42.2 5.4 %collective-permute-done.7 = bf16[16,6144]{1,0:T(8,128)(2,1)S(1)} collective-permute-done((bf16[16,6144]{1,0:T(8,128)(2,1)S(1)}, bf16[16,6144]{1,0:T(8,128)(2,1)S(1)}, u32[]{:S(2)}, u32[]{:S(2)}) %collective-permute-start.7) | collective-permute-done | bytes 196640 | tf_op jit(solution)/shard_map/ppermute | solution.py:176
  47.7 0.1 fusion
  47.8 0.8 %collective-permute-start.8 = (bf16[4,6144]{1,0:T(4,128)(2,1)S(1)}, bf16[4,6144]{1,0:T(4,128)(2,1)S(1)}, u32[]{:S(2)}, u32[]{:S(2)}) collective-permute-start(bf16[4,6144]{1,0:T(4,128)(2,1)S(1)} %get-tuple-element.13), channel_id=1, source_target_pairs={{0,2},{1,3},{2,0},{3,1},{4,6},{5,7},{6,4},{7,5},{8,10},{9,11},{10,... | collective-permute-start | bytes 147464 | tf_op jit(solution)/shard_map/ppermute | solution.py:176
  48.5 2.6 %collective-permute-start.10 = (bf16[4,6144]{1,0:T(4,128)(2,1)S(1)}, bf16[4,6144]{1,0:T(4,128)(2,1)S(1)}, u32[]{:S(2)}, u32[]{:S(2)}) collective-permute-start(bf16[4,6144]{1,0:T(4,128)(2,1)S(1)} %get-tuple-element.14), channel_id=1, source_target_pairs={{0,6},{1,7},{2,4},{3,5},{4,2},{5,3},{6,0},{7,1},{8,14},{9,15},{10,... | collective-permute-start | bytes 147464 | tf_op jit(solution)/shard_map/ppermute | solution.py:176
  51.2 0.1 collective-permute-start.9
  51.3 0.6 %collective-permute-done.8 = bf16[4,6144]{1,0:T(4,128)(2,1)S(1)} collective-permute-done((bf16[4,6144]{1,0:T(4,128)(2,1)S(1)}, bf16[4,6144]{1,0:T(4,128)(2,1)S(1)}, u32[]{:S(2)}, u32[]{:S(2)}) %collective-permute-start.8) | collective-permute-done | bytes 49184 | tf_op jit(solution)/shard_map/ppermute | solution.py:176
  51.9 2.6 %collective-permute-done.10 = bf16[4,6144]{1,0:T(4,128)(2,1)S(1)} collective-permute-done((bf16[4,6144]{1,0:T(4,128)(2,1)S(1)}, bf16[4,6144]{1,0:T(4,128)(2,1)S(1)}, u32[]{:S(2)}, u32[]{:S(2)}) %collective-permute-start.10) | collective-permute-done | bytes 49184 | tf_op jit(solution)/shard_map/ppermute | solution.py:176
  54.5 1.6 %collective-permute-done.9 = bf16[4,6144]{1,0:T(4,128)(2,1)S(1)} collective-permute-done((bf16[4,6144]{1,0:T(4,128)(2,1)S(1)}, bf16[4,6144]{1,0:T(4,128)(2,1)S(1)}, u32[]{:S(2)}, u32[]{:S(2)}) %collective-permute-start.9) | collective-permute-done | bytes 49184 | tf_op jit(solution)/shard_map/ppermute | solution.py:176
  56.2 0.7 %add_convert_fusion.2 = bf16[4,6144]{1,0:T(4,128)(2,1)} fusion(bf16[4,6144]{1,0:T(4,128)(2,1)S(1)} %collective-permute-done.10, bf16[4,6144]{1,0:T(4,128)(2,1)S(1)} %collective-permute-done.9, bf16[4,6144]{1,0:T(4,128)(2,1)S(1)} %collective-permute-done.8, bf16[16,6144]{1,0:T(8,128)(2,1)S(1)} %add_convert_fusion.1), kind=kLoop, calls=%fused_computation.2 | loop fusion | flops 196608 | bytes 245760 | tf_op jit(solution)/shard_map/convert_element_type | solution.py:263
  (3 shorter events, 0.1 us)
Async XLA Ops:
  0.0 18.8 %slice-start = ((s8[31457280]{0:T(1024)(128)(4,1)}), s8[4194304]{0:T(1024)(128)(4,1)S(1)}, s32[]{:S(2)}) async-start(s8[31457280]{0:T(1024)(128)(4,1)} %bitcast.2), calls=%async_computation | async-start | bytes 8388608
  0.0 18.8 %slice-start.1 = ((s8[31457280]{0:T(1024)(128)(4,1)}), s8[4194304]{0:T(1024)(128)(4,1)S(1)}, s32[]{:S(2)}) async-start(s8[31457280]{0:T(1024)(128)(4,1)} %bitcast.2), calls=%async_computation.1 | async-start | bytes 8388608
  0.0 18.8 %slice-start.2 = ((s8[31457280]{0:T(1024)(128)(4,1)}), s8[4194304]{0:T(1024)(128)(4,1)S(1)}, s32[]{:S(2)}) async-start(s8[31457280]{0:T(1024)(128)(4,1)} %bitcast.2), calls=%async_computation.2 | async-start | bytes 8388608
  0.0 18.8 %slice-start.3 = ((s8[31457280]{0:T(1024)(128)(4,1)}), s8[4194304]{0:T(1024)(128)(4,1)S(1)}, s32[]{:S(2)}) async-start(s8[31457280]{0:T(1024)(128)(4,1)} %bitcast.2), calls=%async_computation.3 | async-start | bytes 8388608
  0.0 18.8 %slice-start.4 = ((s8[31457280]{0:T(1024)(128)(4,1)}), s8[4194304]{0:T(1024)(128)(4,1)S(1)}, s32[]{:S(2)}) async-start(s8[31457280]{0:T(1024)(128)(4,1)} %bitcast.2), calls=%async_computation.4 | async-start | bytes 8388608
  0.0 18.8 %slice-start.5 = ((s8[31457280]{0:T(1024)(128)(4,1)}), s8[4194304]{0:T(1024)(128)(4,1)S(1)}, s32[]{:S(2)}) async-start(s8[31457280]{0:T(1024)(128)(4,1)} %bitcast.2), calls=%async_computation.5 | async-start | bytes 8388608
  0.0 18.8 %slice-start.6 = ((s8[31457280]{0:T(1024)(128)(4,1)}), s8[4194304]{0:T(1024)(128)(4,1)S(1)}, s32[]{:S(2)}) async-start(s8[31457280]{0:T(1024)(128)(4,1)} %bitcast.2), calls=%async_computation.6 | async-start | bytes 8388608
  0.0 18.8 %slice-start.7 = ((s8[31457280]{0:T(1024)(128)(4,1)}), s8[2097152]{0:T(1024)(128)(4,1)S(1)}, s32[]{:S(2)}) async-start(s8[31457280]{0:T(1024)(128)(4,1)} %bitcast.2), calls=%async_computation.7 | async-start | bytes 4194304
  1.2 7.4 %collective-permute-start.2 = (bf16[4,6272]{1,0:T(4,128)(2,1)S(1)}, bf16[4,6272]{1,0:T(4,128)(2,1)S(1)}, u32[]{:S(2)}, u32[]{:S(2)}) collective-permute-start(bf16[4,6272]{1,0:T(4,128)(2,1)S(1)} %norm.1.refs_0_), channel_id=1, source_target_pairs={{0,6},{1,7},{2,4},{3,5},{4,2},{5,3},{6,0},{7,1},{8,14},{9,15},{10,... | collective-permute-start | bytes 150536 | tf_op jit(solution)/shard_map/ppermute | solution.py:176
  6.3 5.0 %collective-permute-start.1 = (bf16[4,6272]{1,0:T(4,128)(2,1)S(1)}, bf16[4,6272]{1,0:T(4,128)(2,1)S(1)}, u32[]{:S(2)}, u32[]{:S(2)}) collective-permute-start(bf16[4,6272]{1,0:T(4,128)(2,1)S(1)} %norm.1.refs_0_), channel_id=1, source_target_pairs={{0,4},{1,5},{2,6},{3,7},{4,0},{5,1},{6,2},{7,3},{8,12},{9,13},{10,... | collective-permute-start | bytes 150536 | tf_op jit(solution)/shard_map/ppermute | solution.py:176
  6.3 5.0 %collective-permute-start = (bf16[4,6272]{1,0:T(4,128)(2,1)S(1)}, bf16[4,6272]{1,0:T(4,128)(2,1)S(1)}, u32[]{:S(2)}, u32[]{:S(2)}) collective-permute-start(bf16[4,6272]{1,0:T(4,128)(2,1)S(1)} %norm.1.refs_0_), channel_id=1, source_target_pairs={{0,2},{1,3},{2,0},{3,1},{4,6},{5,7},{6,4},{7,5},{8,10},{9,11},{10,... | collective-permute-start | bytes 150536 | tf_op jit(solution)/shard_map/ppermute | solution.py:176
  11.4 5.9 %collective-permute-start.3 = (bf16[16,6272]{1,0:T(8,128)(2,1)S(1)}, bf16[16,6272]{1,0:T(8,128)(2,1)S(1)}, u32[]{:S(2)}, u32[]{:S(2)}) collective-permute-start(bf16[16,6272]{1,0:T(8,128)(2,1)S(1)} %join.1.after_ref.even_ref), channel_id=1, source_target_pairs={{0,1},{1,0},{2,3},{3,2},{4,5},{5,4},{6,7},{7,6},{8,9},{9,8},{10,11... | collective-permute-start | bytes 602120 | tf_op jit(solution)/shard_map/ppermute | solution.py:176
  13.0 4.3 %collective-permute-start.4 = (bf16[16,6272]{1,0:T(8,128)(2,1)S(1)}, bf16[16,6272]{1,0:T(8,128)(2,1)S(1)}, u32[]{:S(2)}, u32[]{:S(2)}) collective-permute-start(bf16[16,6272]{1,0:T(8,128)(2,1)S(1)} %join.1.after_ref.even_ref), channel_id=1, source_target_pairs={{0,8},{8,0},{1,9},{9,1},{2,10},{10,2},{3,11},{11,3},{4,12},{12,4},... | collective-permute-start | bytes 602120 | tf_op jit(solution)/shard_map/ppermute | solution.py:171
  17.3 1.4 %collective-permute-start.5 = (bf16[16,6272]{1,0:T(8,128)(2,1)S(1)}, bf16[16,6272]{1,0:T(8,128)(2,1)S(1)}, u32[]{:S(2)}, u32[]{:S(2)}) collective-permute-start(bf16[16,6272]{1,0:T(8,128)(2,1)S(1)} %collective-permute-done.3.odd_ref), channel_id=1, source_target_pairs={{0,8},{8,0},{1,9},{9,1},{2,10},{10,2},{3,11},{11,3},{4,12},{12,4},... | collective-permute-start | bytes 602120 | tf_op jit(solution)/shard_map/ppermute | solution.py:171
  38.7 1.8 %collective-permute-start.6 = (bf16[32,6144]{1,0:T(8,128)(2,1)S(1)}, bf16[32,6144]{1,0:T(8,128)(2,1)S(1)}, u32[]{:S(2)}, u32[]{:S(2)}) collective-permute-start(bf16[32,6144]{1,0:T(8,128)(2,1)S(1)} %get-tuple-element.12), channel_id=1, source_target_pairs={{0,8},{8,0},{1,9},{9,1},{2,10},{10,2},{3,11},{11,3},{4,12},{12,4},... | collective-permute-start | bytes 1179656 | tf_op jit(solution)/shard_map/ppermute | solution.py:171
  40.6 7.0 %collective-permute-start.7 = (bf16[16,6144]{1,0:T(8,128)(2,1)S(1)}, bf16[16,6144]{1,0:T(8,128)(2,1)S(1)}, u32[]{:S(2)}, u32[]{:S(2)}) collective-permute-start(bf16[16,6144]{1,0:T(8,128)(2,1)S(1)} %slice.25), channel_id=1, source_target_pairs={{0,1},{1,0},{2,3},{3,2},{4,5},{5,4},{6,7},{7,6},{8,9},{9,8},{10,11... | collective-permute-start | bytes 589832 | tf_op jit(solution)/shard_map/ppermute | solution.py:176
  47.8 4.2 %collective-permute-start.8 = (bf16[4,6144]{1,0:T(4,128)(2,1)S(1)}, bf16[4,6144]{1,0:T(4,128)(2,1)S(1)}, u32[]{:S(2)}, u32[]{:S(2)}) collective-permute-start(bf16[4,6144]{1,0:T(4,128)(2,1)S(1)} %get-tuple-element.13), channel_id=1, source_target_pairs={{0,2},{1,3},{2,0},{3,1},{4,6},{5,7},{6,4},{7,5},{8,10},{9,11},{10,... | collective-permute-start | bytes 147464 | tf_op jit(solution)/shard_map/ppermute | solution.py:176
  48.5 6.0 %collective-permute-start.10 = (bf16[4,6144]{1,0:T(4,128)(2,1)S(1)}, bf16[4,6144]{1,0:T(4,128)(2,1)S(1)}, u32[]{:S(2)}, u32[]{:S(2)}) collective-permute-start(bf16[4,6144]{1,0:T(4,128)(2,1)S(1)} %get-tuple-element.14), channel_id=1, source_target_pairs={{0,6},{1,7},{2,4},{3,5},{4,2},{5,3},{6,0},{7,1},{8,14},{9,15},{10,... | collective-permute-start | bytes 147464 | tf_op jit(solution)/shard_map/ppermute | solution.py:176
  51.2 5.0 %collective-permute-start.9 = (bf16[4,6144]{1,0:T(4,128)(2,1)S(1)}, bf16[4,6144]{1,0:T(4,128)(2,1)S(1)}, u32[]{:S(2)}, u32[]{:S(2)}) collective-permute-start(bf16[4,6144]{1,0:T(4,128)(2,1)S(1)} %get-tuple-element.15), channel_id=1, source_target_pairs={{0,4},{1,5},{2,6},{3,7},{4,0},{5,1},{6,2},{7,3},{8,12},{9,13},{10,... | collective-permute-start | bytes 147464 | tf_op jit(solution)/shard_map/ppermute | solution.py:176

commit v5 on v4

--- a/solution.py
+++ b/solution.py
@@ -84,7 +84,7 @@
 
 def expert_kernel(
     devices, up_block, down_block, even_ref, odd_ref, other_even_ref, other_odd_ref, gate_ref, held_ref,
-    w_up_ref, w_down_ref, kept_ref, sent_ref, x, hidden, slots, sems,
+    w_up_ref, w_down_ref, kept_even_ref, kept_odd_ref, sent_even_ref, sent_odd_ref, x, hidden, slots, sems,
 ):
     pieces = (even_ref, odd_ref, other_even_ref, other_odd_ref)
     quarter = even_ref.shape[0]
@@ -144,14 +144,14 @@
         hidden[:, columns] = (gate / (1.0 + jnp.exp(-gate)) * up).astype(hidden.dtype)
 
     activations = hidden[...]
+    targets = (kept_even_ref, kept_odd_ref, sent_even_ref, sent_odd_ref)
 
     def finish(block, first):
         out = jnp.dot(activations, block, preferred_element_type=jnp.float32)
         columns = pl.ds(first, down_block)
-        for i, weight in enumerate(weights):
-            target = (kept_ref, sent_ref)[i // 2]
+        for i, (weight, target) in enumerate(zip(weights, targets)):
             piece = out[i * quarter : (i + 1) * quarter] * weight
-            target[i % 2 * quarter : (i % 2 + 1) * quarter, columns] = piece.astype(target.dtype)
+            target[:, columns] = piece.astype(target.dtype)
 
     for j in range(max(helds, downs)):
         if j < helds:
@@ -222,11 +222,11 @@
     other_odd = swap_sides(odd)
 
     padded = max(2 * half, MIN_ROWS)
-    kept, sent = pl.pallas_call(
+    kept_even, kept_odd, sent_even, sent_odd = pl.pallas_call(
         functools.partial(expert_kernel, devices, up_block, down_block),
         in_specs=[VMEM] * 6 + [HBM] * 2,
-        out_specs=[VMEM] * 2,
-        out_shape=[jax.ShapeDtypeStruct((half, width), dtype)] * 2,
+        out_specs=[VMEM] * 4,
+        out_shape=[jax.ShapeDtypeStruct((half // 2, width), dtype)] * 4,
         scratch_shapes=[
             pltpu.VMEM((padded, width), dtype),
             pltpu.VMEM((padded, units), dtype),
@@ -254,9 +254,8 @@
     def add(values):
         return sum(v.astype(jnp.float32) for v in values)
 
-    summed = add([kept, swap_sides(sent)]).astype(dtype)
-    middle = half // 2
-    plane = add([summed[:middle], swap_chips(summed[middle:], 1)]).astype(dtype)
+    odd_sum = add([kept_odd, swap_sides(sent_odd)]).astype(dtype)
+    plane = add([kept_even, swap_sides(sent_even), swap_chips(odd_sum, 1)]).astype(dtype)
     arrived = [
         swap_chips(plane[d // 2 * rows : (d // 2 + 1) * rows], d) for d in range(2, chips, 2)
     ]

time: 57 us -> 56.7 us (level)
  waiting for transfers between devices: 19.4 us -> 18.7 us
    ppermute x3 -> x4, waiting for transfers between devices: 3.04 us -> 2.38 us  [swap_sides(): lax.ppermute(values, 'side', [(i, sides - 1 - i) for i in range(sides)])]
  transfers between devices with their start and end apart: 11 -> 12, of which waited for: 9 -> 9; matrix products, arithmetic and copies ran while one was open for 0% -> 0% of each run, Pallas kernels for 5% -> 5%
where the time goes in v5:
time: 56.7 us; the launch traced here: 56.5 us
  Pallas kernels  23.7 us (42%)
  waiting for transfers between devices  18.7 us (33%)
  starting transfers between devices  13.1 us (23%)
  other arithmetic  0.8 us (1%)
    pallas_call x1, Pallas kernels, shards(): pl.pallas_call(functools.partial(expert_kernel, devices, up_block, down_b...  19.9 us
    ppermute x8, waiting for transfers between devices, swap_chips(): lax.ppermute(values, 'attn', [(i, i ^ distance) for i in range(chips)])  16.4 us
    ppermute x8, starting transfers between devices, swap_chips(): lax.ppermute(values, 'attn', [(i, i ^ distance) for i in range(chips)])  12.5 us
    pallas_call x1, Pallas kernels, shards(): pl.pallas_call(fetch_kernel, in_specs=[HBM] * 2, out_specs=VMEM, out_shap...  2.58 us
    ppermute x4, waiting for transfers between devices, swap_sides(): lax.ppermute(values, 'side', [(i, sides - 1 - i) for i in range(sides)])  2.38 us
    pallas_call x1, Pallas kernels, shards(): pl.pallas_call(norm_kernel, in_specs=[HBM] * 4, out_specs=VMEM, out_shape...  1.15 us
  transfers between devices with their start and end apart: 12, of which 9 were waited for; matrix products, arithmetic and copies ran while one was open for 0% of the time, Pallas kernels for 5%

profile of v5, /device:TPU:0, one launch (start us, length us, event | category | flops | bytes accessed | tf_op | source)
XLA Modules:
  0.0 56.5 jit_solution(14814601768981066569)
XLA Ops:
  0.0 0.0 slice-start
  0.0 0.0 slice-start.1
  0.0 0.0 slice-start.2
  0.0 0.0 slice-start.3
  0.0 0.0 slice-start.4
  0.0 0.0 slice-start.5
  0.0 0.0 slice-start.6
  0.0 0.0 slice-start.7
  0.0 1.1 %norm.1.refs_0_ = bf16[4,6272]{1,0:T(4,128)(2,1)S(1)} custom-call(bf16[4,6144]{1,0:T(4,128)(2,1)} %refs_0_.1, bf16[6144]{0:T(1024)(128)(2,1)} %refs_1_.1, s32[2,4]{1,0:T(2,128)} %bitcast.4, bf16[2,4]{1,0:T(2,128)(2,1)} %bitcast.5), custom_call_target="tpu_custom_call" | custom-call | flops 99999997952 | bytes 1000000 | tf_op jit(solution)/shard_map/norm/pallas_call | solution.py:194
  1.2 5.1 %collective-permute-start.2 = (bf16[4,6272]{1,0:T(4,128)(2,1)S(1)}, bf16[4,6272]{1,0:T(4,128)(2,1)S(1)}, u32[]{:S(2)}, u32[]{:S(2)}) collective-permute-start(bf16[4,6272]{1,0:T(4,128)(2,1)S(1)} %norm.1.refs_0_), channel_id=1, source_target_pairs={{0,6},{1,7},{2,4},{3,5},{4,2},{5,3},{6,0},{7,1},{8,14},{9,15},{10,... | collective-permute-start | bytes 150536 | tf_op jit(solution)/shard_map/ppermute | solution.py:176
  6.3 0.0 collective-permute-start.1
  6.3 0.6 %collective-permute-start = (bf16[4,6272]{1,0:T(4,128)(2,1)S(1)}, bf16[4,6272]{1,0:T(4,128)(2,1)S(1)}, u32[]{:S(2)}, u32[]{:S(2)}) collective-permute-start(bf16[4,6272]{1,0:T(4,128)(2,1)S(1)} %norm.1.refs_0_), channel_id=1, source_target_pairs={{0,2},{1,3},{2,0},{3,1},{4,6},{5,7},{6,4},{7,5},{8,10},{9,11},{10,... | collective-permute-start | bytes 150536 | tf_op jit(solution)/shard_map/ppermute | solution.py:176
  7.0 1.6 %collective-permute-done.2.refs_3_ = bf16[4,6272]{1,0:T(4,128)(2,1)S(1)} collective-permute-done((bf16[4,6272]{1,0:T(4,128)(2,1)S(1)}, bf16[4,6272]{1,0:T(4,128)(2,1)S(1)}, u32[]{:S(2)}, u32[]{:S(2)}) %collective-permute-start.2) | collective-permute-done | bytes 50208 | tf_op jit(solution)/shard_map/ppermute | solution.py:176
  8.6 2.7 %collective-permute-done.1.refs_2_ = bf16[4,6272]{1,0:T(4,128)(2,1)S(1)} collective-permute-done((bf16[4,6272]{1,0:T(4,128)(2,1)S(1)}, bf16[4,6272]{1,0:T(4,128)(2,1)S(1)}, u32[]{:S(2)}, u32[]{:S(2)}) %collective-permute-start.1) | collective-permute-done | bytes 50208 | tf_op jit(solution)/shard_map/ppermute | solution.py:176
  11.3 0.0 collective-permute-done.refs_1_
  11.3 0.1 join.1.after_ref.even_ref
  11.4 1.6 %collective-permute-start.3 = (bf16[16,6272]{1,0:T(8,128)(2,1)S(1)}, bf16[16,6272]{1,0:T(8,128)(2,1)S(1)}, u32[]{:S(2)}, u32[]{:S(2)}) collective-permute-start(bf16[16,6272]{1,0:T(8,128)(2,1)S(1)} %join.1.after_ref.even_ref), channel_id=1, source_target_pairs={{0,1},{1,0},{2,3},{3,2},{4,5},{5,4},{6,7},{7,6},{8,9},{9,8},{10,11... | collective-permute-start | bytes 602120 | tf_op jit(solution)/shard_map/ppermute | solution.py:176
  13.0 0.0 collective-permute-start.4
  13.0 2.6 %fetch.1.held_ref = bf16[2560,1024]{1,0:T(8,128)(2,1)S(1)} custom-call(bf16[16,6272]{1,0:T(8,128)(2,1)S(1)} %join.1.after_ref.even_ref, bf16[2560,6144]{1,0:T(8,128)(2,1)} %w_down_ref.3), custom_call_target="tpu_custom_call" | custom-call | bytes 5242880 | tf_op jit(solution)/shard_map/fetch/pallas_call | solution.py:209
  15.6 1.7 %collective-permute-done.3.odd_ref = bf16[16,6272]{1,0:T(8,128)(2,1)S(1)} collective-permute-done((bf16[16,6272]{1,0:T(8,128)(2,1)S(1)}, bf16[16,6272]{1,0:T(8,128)(2,1)S(1)}, u32[]{:S(2)}, u32[]{:S(2)}) %collective-permute-start.3) | collective-permute-done | bytes 200736 | tf_op jit(solution)/shard_map/ppermute | solution.py:176
  17.3 0.0 collective-permute-start.5
  17.3 0.0 collective-permute-done.4.other_even_ref
  17.3 1.4 %collective-permute-done.5.other_odd_ref = bf16[16,6272]{1,0:T(8,128)(2,1)S(1)} collective-permute-done((bf16[16,6272]{1,0:T(8,128)(2,1)S(1)}, bf16[16,6272]{1,0:T(8,128)(2,1)S(1)}, u32[]{:S(2)}, u32[]{:S(2)}) %collective-permute-start.5) | collective-permute-done | bytes 200736 | tf_op jit(solution)/shard_map/ppermute | solution.py:171
  18.8 0.0 slice-done
  18.8 0.0 slice-done.1
  18.8 0.0 slice-done.2
  18.8 0.0 slice-done.3
  18.8 0.0 slice-done.4
  18.8 0.0 slice-done.5
  18.8 0.0 slice-done.6
  18.8 0.0 slice-done.7
  18.8 19.9 %experts.1 = (bf16[16,6144]{1,0:T(8,128)(2,1)S(1)}, bf16[16,6144]{1,0:T(8,128)(2,1)S(1)}, bf16[16,6144]{1,0:T(8,128)(2,1)S(1)}, bf16[16,6144]{1,0:T(8,128)(2,1)S(1)}) custom-call(bf16[16,6272]{1,0:T(8,128)(2,1)S(1)} %join.1.after_ref.even_ref, bf16[16,6272]{1,0:T(8,128)(2,1)S(1)} %collective-permute-done.3.odd_ref, ...), custom_call_target="tpu_custom_call" | custom-call | flops 6039797760 | bytes 57671680 | tf_op jit(solution)/shard_map/experts/pallas_call | solution.py:225
  38.7 0.2 collective-permute-start.7
  38.9 0.4 collective-permute-start.6
  39.3 0.9 %collective-permute-done.7 = bf16[16,6144]{1,0:T(8,128)(2,1)S(1)} collective-permute-done((bf16[16,6144]{1,0:T(8,128)(2,1)S(1)}, bf16[16,6144]{1,0:T(8,128)(2,1)S(1)}, u32[]{:S(2)}, u32[]{:S(2)}) %collective-permute-start.7) | collective-permute-done | bytes 196640 | tf_op jit(solution)/shard_map/ppermute | solution.py:171
  40.2 0.1 add_convert_fusion.1
  40.3 1.6 %collective-permute-start.8 = (bf16[16,6144]{1,0:T(8,128)(2,1)S(1)}, bf16[16,6144]{1,0:T(8,128)(2,1)S(1)}, u32[]{:S(2)}, u32[]{:S(2)}) collective-permute-start(bf16[16,6144]{1,0:T(8,128)(2,1)S(1)} %add_convert_fusion.1), channel_id=1, source_target_pairs={{0,1},{1,0},{2,3},{3,2},{4,5},{5,4},{6,7},{7,6},{8,9},{9,8},{10,11... | collective-permute-start | bytes 589832 | tf_op jit(solution)/shard_map/ppermute | solution.py:176
  41.9 0.0 collective-permute-done.6
  41.9 5.4 %collective-permute-done.8 = bf16[16,6144]{1,0:T(8,128)(2,1)S(1)} collective-permute-done((bf16[16,6144]{1,0:T(8,128)(2,1)S(1)}, bf16[16,6144]{1,0:T(8,128)(2,1)S(1)}, u32[]{:S(2)}, u32[]{:S(2)}) %collective-permute-start.8) | collective-permute-done | bytes 196640 | tf_op jit(solution)/shard_map/ppermute | solution.py:176
  47.3 0.1 add_convert_fusion
  47.4 0.1 fusion
  47.5 0.8 %collective-permute-start.9 = (bf16[4,6144]{1,0:T(4,128)(2,1)S(1)}, bf16[4,6144]{1,0:T(4,128)(2,1)S(1)}, u32[]{:S(2)}, u32[]{:S(2)}) collective-permute-start(bf16[4,6144]{1,0:T(4,128)(2,1)S(1)} %get-tuple-element.17), channel_id=1, source_target_pairs={{0,2},{1,3},{2,0},{3,1},{4,6},{5,7},{6,4},{7,5},{8,10},{9,11},{10,... | collective-permute-start | bytes 147464 | tf_op jit(solution)/shard_map/ppermute | solution.py:176
  48.2 2.7 %collective-permute-start.11 = (bf16[4,6144]{1,0:T(4,128)(2,1)S(1)}, bf16[4,6144]{1,0:T(4,128)(2,1)S(1)}, u32[]{:S(2)}, u32[]{:S(2)}) collective-permute-start(bf16[4,6144]{1,0:T(4,128)(2,1)S(1)} %get-tuple-element.18), channel_id=1, source_target_pairs={{0,6},{1,7},{2,4},{3,5},{4,2},{5,3},{6,0},{7,1},{8,14},{9,15},{10,... | collective-permute-start | bytes 147464 | tf_op jit(solution)/shard_map/ppermute | solution.py:176
  50.9 0.1 collective-permute-start.10
  51.0 0.6 %collective-permute-done.9 = bf16[4,6144]{1,0:T(4,128)(2,1)S(1)} collective-permute-done((bf16[4,6144]{1,0:T(4,128)(2,1)S(1)}, bf16[4,6144]{1,0:T(4,128)(2,1)S(1)}, u32[]{:S(2)}, u32[]{:S(2)}) %collective-permute-start.9) | collective-permute-done | bytes 49184 | tf_op jit(solution)/shard_map/ppermute | solution.py:176
  51.6 2.6 %collective-permute-done.11 = bf16[4,6144]{1,0:T(4,128)(2,1)S(1)} collective-permute-done((bf16[4,6144]{1,0:T(4,128)(2,1)S(1)}, bf16[4,6144]{1,0:T(4,128)(2,1)S(1)}, u32[]{:S(2)}, u32[]{:S(2)}) %collective-permute-start.11) | collective-permute-done | bytes 49184 | tf_op jit(solution)/shard_map/ppermute | solution.py:176
  54.2 1.7 %collective-permute-done.10 = bf16[4,6144]{1,0:T(4,128)(2,1)S(1)} collective-permute-done((bf16[4,6144]{1,0:T(4,128)(2,1)S(1)}, bf16[4,6144]{1,0:T(4,128)(2,1)S(1)}, u32[]{:S(2)}, u32[]{:S(2)}) %collective-permute-start.10) | collective-permute-done | bytes 49184 | tf_op jit(solution)/shard_map/ppermute | solution.py:176
  55.9 0.7 %add_convert_fusion.2 = bf16[4,6144]{1,0:T(4,128)(2,1)} fusion(bf16[4,6144]{1,0:T(4,128)(2,1)S(1)} %collective-permute-done.11, bf16[4,6144]{1,0:T(4,128)(2,1)S(1)} %collective-permute-done.10, bf16[4,6144]{1,0:T(4,128)(2,1)S(1)} %collective-permute-done.9, bf16[16,6144]{1,0:T(8,128)(2,1)S(1)} %add_convert_fusion), kind=kLoop, calls=%fused_computation.2 | loop fusion | flops 196608 | bytes 245760 | tf_op jit(solution)/shard_map/convert_element_type | solution.py:262
  (1 shorter events, 0.0 us)
Async XLA Ops:
  0.0 18.8 %slice-start = ((s8[31457280]{0:T(1024)(128)(4,1)}), s8[4194304]{0:T(1024)(128)(4,1)S(1)}, s32[]{:S(2)}) async-start(s8[31457280]{0:T(1024)(128)(4,1)} %bitcast.2), calls=%async_computation | async-start | bytes 8388608
  0.0 18.8 %slice-start.1 = ((s8[31457280]{0:T(1024)(128)(4,1)}), s8[4194304]{0:T(1024)(128)(4,1)S(1)}, s32[]{:S(2)}) async-start(s8[31457280]{0:T(1024)(128)(4,1)} %bitcast.2), calls=%async_computation.1 | async-start | bytes 8388608
  0.0 18.8 %slice-start.2 = ((s8[31457280]{0:T(1024)(128)(4,1)}), s8[4194304]{0:T(1024)(128)(4,1)S(1)}, s32[]{:S(2)}) async-start(s8[31457280]{0:T(1024)(128)(4,1)} %bitcast.2), calls=%async_computation.2 | async-start | bytes 8388608
  0.0 18.8 %slice-start.3 = ((s8[31457280]{0:T(1024)(128)(4,1)}), s8[4194304]{0:T(1024)(128)(4,1)S(1)}, s32[]{:S(2)}) async-start(s8[31457280]{0:T(1024)(128)(4,1)} %bitcast.2), calls=%async_computation.3 | async-start | bytes 8388608
  0.0 18.8 %slice-start.4 = ((s8[31457280]{0:T(1024)(128)(4,1)}), s8[4194304]{0:T(1024)(128)(4,1)S(1)}, s32[]{:S(2)}) async-start(s8[31457280]{0:T(1024)(128)(4,1)} %bitcast.2), calls=%async_computation.4 | async-start | bytes 8388608
  0.0 18.8 %slice-start.5 = ((s8[31457280]{0:T(1024)(128)(4,1)}), s8[4194304]{0:T(1024)(128)(4,1)S(1)}, s32[]{:S(2)}) async-start(s8[31457280]{0:T(1024)(128)(4,1)} %bitcast.2), calls=%async_computation.5 | async-start | bytes 8388608
  0.0 18.8 %slice-start.6 = ((s8[31457280]{0:T(1024)(128)(4,1)}), s8[4194304]{0:T(1024)(128)(4,1)S(1)}, s32[]{:S(2)}) async-start(s8[31457280]{0:T(1024)(128)(4,1)} %bitcast.2), calls=%async_computation.6 | async-start | bytes 8388608
  0.0 18.8 %slice-start.7 = ((s8[31457280]{0:T(1024)(128)(4,1)}), s8[2097152]{0:T(1024)(128)(4,1)S(1)}, s32[]{:S(2)}) async-start(s8[31457280]{0:T(1024)(128)(4,1)} %bitcast.2), calls=%async_computation.7 | async-start | bytes 4194304
  1.2 7.4 %collective-permute-start.2 = (bf16[4,6272]{1,0:T(4,128)(2,1)S(1)}, bf16[4,6272]{1,0:T(4,128)(2,1)S(1)}, u32[]{:S(2)}, u32[]{:S(2)}) collective-permute-start(bf16[4,6272]{1,0:T(4,128)(2,1)S(1)} %norm.1.refs_0_), channel_id=1, source_target_pairs={{0,6},{1,7},{2,4},{3,5},{4,2},{5,3},{6,0},{7,1},{8,14},{9,15},{10,... | collective-permute-start | bytes 150536 | tf_op jit(solution)/shard_map/ppermute | solution.py:176
  6.3 5.0 %collective-permute-start.1 = (bf16[4,6272]{1,0:T(4,128)(2,1)S(1)}, bf16[4,6272]{1,0:T(4,128)(2,1)S(1)}, u32[]{:S(2)}, u32[]{:S(2)}) collective-permute-start(bf16[4,6272]{1,0:T(4,128)(2,1)S(1)} %norm.1.refs_0_), channel_id=1, source_target_pairs={{0,4},{1,5},{2,6},{3,7},{4,0},{5,1},{6,2},{7,3},{8,12},{9,13},{10,... | collective-permute-start | bytes 150536 | tf_op jit(solution)/shard_map/ppermute | solution.py:176
  6.3 5.0 %collective-permute-start = (bf16[4,6272]{1,0:T(4,128)(2,1)S(1)}, bf16[4,6272]{1,0:T(4,128)(2,1)S(1)}, u32[]{:S(2)}, u32[]{:S(2)}) collective-permute-start(bf16[4,6272]{1,0:T(4,128)(2,1)S(1)} %norm.1.refs_0_), channel_id=1, source_target_pairs={{0,2},{1,3},{2,0},{3,1},{4,6},{5,7},{6,4},{7,5},{8,10},{9,11},{10,... | collective-permute-start | bytes 150536 | tf_op jit(solution)/shard_map/ppermute | solution.py:176
  11.4 5.9 %collective-permute-start.3 = (bf16[16,6272]{1,0:T(8,128)(2,1)S(1)}, bf16[16,6272]{1,0:T(8,128)(2,1)S(1)}, u32[]{:S(2)}, u32[]{:S(2)}) collective-permute-start(bf16[16,6272]{1,0:T(8,128)(2,1)S(1)} %join.1.after_ref.even_ref), channel_id=1, source_target_pairs={{0,1},{1,0},{2,3},{3,2},{4,5},{5,4},{6,7},{7,6},{8,9},{9,8},{10,11... | collective-permute-start | bytes 602120 | tf_op jit(solution)/shard_map/ppermute | solution.py:176
  13.0 4.3 %collective-permute-start.4 = (bf16[16,6272]{1,0:T(8,128)(2,1)S(1)}, bf16[16,6272]{1,0:T(8,128)(2,1)S(1)}, u32[]{:S(2)}, u32[]{:S(2)}) collective-permute-start(bf16[16,6272]{1,0:T(8,128)(2,1)S(1)} %join.1.after_ref.even_ref), channel_id=1, source_target_pairs={{0,8},{8,0},{1,9},{9,1},{2,10},{10,2},{3,11},{11,3},{4,12},{12,4},... | collective-permute-start | bytes 602120 | tf_op jit(solution)/shard_map/ppermute | solution.py:171
  17.3 1.4 %collective-permute-start.5 = (bf16[16,6272]{1,0:T(8,128)(2,1)S(1)}, bf16[16,6272]{1,0:T(8,128)(2,1)S(1)}, u32[]{:S(2)}, u32[]{:S(2)}) collective-permute-start(bf16[16,6272]{1,0:T(8,128)(2,1)S(1)} %collective-permute-done.3.odd_ref), channel_id=1, source_target_pairs={{0,8},{8,0},{1,9},{9,1},{2,10},{10,2},{3,11},{11,3},{4,12},{12,4},... | collective-permute-start | bytes 602120 | tf_op jit(solution)/shard_map/ppermute | solution.py:171
  38.7 1.5 %collective-permute-start.7 = (bf16[16,6144]{1,0:T(8,128)(2,1)S(1)}, bf16[16,6144]{1,0:T(8,128)(2,1)S(1)}, u32[]{:S(2)}, u32[]{:S(2)}) collective-permute-start(bf16[16,6144]{1,0:T(8,128)(2,1)S(1)} %get-tuple-element.16), channel_id=1, source_target_pairs={{0,8},{8,0},{1,9},{9,1},{2,10},{10,2},{3,11},{11,3},{4,12},{12,4},... | collective-permute-start | bytes 589832 | tf_op jit(solution)/shard_map/ppermute | solution.py:171
  38.9 3.0 %collective-permute-start.6 = (bf16[16,6144]{1,0:T(8,128)(2,1)S(1)}, bf16[16,6144]{1,0:T(8,128)(2,1)S(1)}, u32[]{:S(2)}, u32[]{:S(2)}) collective-permute-start(bf16[16,6144]{1,0:T(8,128)(2,1)S(1)} %get-tuple-element.14), channel_id=1, source_target_pairs={{0,8},{8,0},{1,9},{9,1},{2,10},{10,2},{3,11},{11,3},{4,12},{12,4},... | collective-permute-start | bytes 589832 | tf_op jit(solution)/shard_map/ppermute | solution.py:171
  40.3 7.0 %collective-permute-start.8 = (bf16[16,6144]{1,0:T(8,128)(2,1)S(1)}, bf16[16,6144]{1,0:T(8,128)(2,1)S(1)}, u32[]{:S(2)}, u32[]{:S(2)}) collective-permute-start(bf16[16,6144]{1,0:T(8,128)(2,1)S(1)} %add_convert_fusion.1), channel_id=1, source_target_pairs={{0,1},{1,0},{2,3},{3,2},{4,5},{5,4},{6,7},{7,6},{8,9},{9,8},{10,11... | collective-permute-start | bytes 589832 | tf_op jit(solution)/shard_map/ppermute | solution.py:176
  47.5 4.2 %collective-permute-start.9 = (bf16[4,6144]{1,0:T(4,128)(2,1)S(1)}, bf16[4,6144]{1,0:T(4,128)(2,1)S(1)}, u32[]{:S(2)}, u32[]{:S(2)}) collective-permute-start(bf16[4,6144]{1,0:T(4,128)(2,1)S(1)} %get-tuple-element.17), channel_id=1, source_target_pairs={{0,2},{1,3},{2,0},{3,1},{4,6},{5,7},{6,4},{7,5},{8,10},{9,11},{10,... | collective-permute-start | bytes 147464 | tf_op jit(solution)/shard_map/ppermute | solution.py:176
  48.2 6.0 %collective-permute-start.11 = (bf16[4,6144]{1,0:T(4,128)(2,1)S(1)}, bf16[4,6144]{1,0:T(4,128)(2,1)S(1)}, u32[]{:S(2)}, u32[]{:S(2)}) collective-permute-start(bf16[4,6144]{1,0:T(4,128)(2,1)S(1)} %get-tuple-element.18), channel_id=1, source_target_pairs={{0,6},{1,7},{2,4},{3,5},{4,2},{5,3},{6,0},{7,1},{8,14},{9,15},{10,... | collective-permute-start | bytes 147464 | tf_op jit(solution)/shard_map/ppermute | solution.py:176
  50.9 5.0 %collective-permute-start.10 = (bf16[4,6144]{1,0:T(4,128)(2,1)S(1)}, bf16[4,6144]{1,0:T(4,128)(2,1)S(1)}, u32[]{:S(2)}, u32[]{:S(2)}) collective-permute-start(bf16[4,6144]{1,0:T(4,128)(2,1)S(1)} %get-tuple-element.19), channel_id=1, source_target_pairs={{0,4},{1,5},{2,6},{3,7},{4,0},{5,1},{6,2},{7,3},{8,12},{9,13},{10,... | collective-permute-start | bytes 147464 | tf_op jit(solution)/shard_map/ppermute | solution.py:176

commit v6 on v5

--- a/solution.py
+++ b/solution.py
@@ -153,9 +153,11 @@
             piece = out[i * quarter : (i + 1) * quarter] * weight
             target[:, columns] = piece.astype(target.dtype)
 
-    for j in range(max(helds, downs)):
-        if j < helds:
-            finish(held_ref[:, j * down_block : (j + 1) * down_block], j * down_block)
+    late = max(downs - helds, 0)
+    for j in range(max(late + helds, downs)):
+        if j >= late:
+            first = (j - late) * down_block
+            finish(held_ref[:, first : first + down_block], first)
         if j < downs:
             copy(ups + j).wait()
             finish(slot(ups + j)[...], (helds + j) * down_block)

time: 56.7 us -> 56.6 us (level)
  no operation moved by 1% of the time
where the time goes in v6:
time: 56.6 us; the launch traced here: 56.4 us
  Pallas kernels  23.6 us (42%)
  waiting for transfers between devices  18.7 us (33%)
  starting transfers between devices  13.1 us (23%)
  other arithmetic  0.8 us (1%)
    pallas_call x1, Pallas kernels, shards(): pl.pallas_call(functools.partial(expert_kernel, devices, up_block, down_b...  19.8 us
    ppermute x8, waiting for transfers between devices, swap_chips(): lax.ppermute(values, 'attn', [(i, i ^ distance) for i in range(chips)])  16.4 us
    ppermute x8, starting transfers between devices, swap_chips(): lax.ppermute(values, 'attn', [(i, i ^ distance) for i in range(chips)])  12.5 us
    pallas_call x1, Pallas kernels, shards(): pl.pallas_call(fetch_kernel, in_specs=[HBM] * 2, out_specs=VMEM, out_shap...  2.58 us
    ppermute x4, waiting for transfers between devices, swap_sides(): lax.ppermute(values, 'side', [(i, sides - 1 - i) for i in range(sides)])  2.38 us
    pallas_call x1, Pallas kernels, shards(): pl.pallas_call(norm_kernel, in_specs=[HBM] * 4, out_specs=VMEM, out_shape...  1.15 us
  transfers between devices with their start and end apart: 12, of which 9 were waited for; matrix products, arithmetic and copies ran while one was open for 0% of the time, Pallas kernels for 5%

profile of v6, /device:TPU:0, one launch (start us, length us, event | category | flops | bytes accessed | tf_op | source)
XLA Modules:
  0.0 56.4 jit_solution(5874266432601141660)
XLA Ops:
  0.0 0.0 slice-start
  0.0 0.0 slice-start.1
  0.0 0.0 slice-start.2
  0.0 0.0 slice-start.3
  0.0 0.0 slice-start.4
  0.0 0.0 slice-start.5
  0.0 0.0 slice-start.6
  0.0 0.0 slice-start.7
  0.0 1.1 %norm.1.refs_0_ = bf16[4,6272]{1,0:T(4,128)(2,1)S(1)} custom-call(bf16[4,6144]{1,0:T(4,128)(2,1)} %refs_0_.1, bf16[6144]{0:T(1024)(128)(2,1)} %refs_1_.1, s32[2,4]{1,0:T(2,128)} %bitcast.4, bf16[2,4]{1,0:T(2,128)(2,1)} %bitcast.5), custom_call_target="tpu_custom_call" | custom-call | flops 99999997952 | bytes 1000000 | tf_op jit(solution)/shard_map/norm/pallas_call | solution.py:196
  1.2 5.1 %collective-permute-start.2 = (bf16[4,6272]{1,0:T(4,128)(2,1)S(1)}, bf16[4,6272]{1,0:T(4,128)(2,1)S(1)}, u32[]{:S(2)}, u32[]{:S(2)}) collective-permute-start(bf16[4,6272]{1,0:T(4,128)(2,1)S(1)} %norm.1.refs_0_), channel_id=1, source_target_pairs={{0,6},{1,7},{2,4},{3,5},{4,2},{5,3},{6,0},{7,1},{8,14},{9,15},{10,... | collective-permute-start | bytes 150536 | tf_op jit(solution)/shard_map/ppermute | solution.py:178
  6.3 0.0 collective-permute-start.1
  6.3 0.6 %collective-permute-start = (bf16[4,6272]{1,0:T(4,128)(2,1)S(1)}, bf16[4,6272]{1,0:T(4,128)(2,1)S(1)}, u32[]{:S(2)}, u32[]{:S(2)}) collective-permute-start(bf16[4,6272]{1,0:T(4,128)(2,1)S(1)} %norm.1.refs_0_), channel_id=1, source_target_pairs={{0,2},{1,3},{2,0},{3,1},{4,6},{5,7},{6,4},{7,5},{8,10},{9,11},{10,... | collective-permute-start | bytes 150536 | tf_op jit(solution)/shard_map/ppermute | solution.py:178
  7.0 1.6 %collective-permute-done.2.refs_3_ = bf16[4,6272]{1,0:T(4,128)(2,1)S(1)} collective-permute-done((bf16[4,6272]{1,0:T(4,128)(2,1)S(1)}, bf16[4,6272]{1,0:T(4,128)(2,1)S(1)}, u32[]{:S(2)}, u32[]{:S(2)}) %collective-permute-start.2) | collective-permute-done | bytes 50208 | tf_op jit(solution)/shard_map/ppermute | solution.py:178
  8.6 2.7 %collective-permute-done.1.refs_2_ = bf16[4,6272]{1,0:T(4,128)(2,1)S(1)} collective-permute-done((bf16[4,6272]{1,0:T(4,128)(2,1)S(1)}, bf16[4,6272]{1,0:T(4,128)(2,1)S(1)}, u32[]{:S(2)}, u32[]{:S(2)}) %collective-permute-start.1) | collective-permute-done | bytes 50208 | tf_op jit(solution)/shard_map/ppermute | solution.py:178
  11.3 0.0 collective-permute-done.refs_1_
  11.3 0.1 join.1.after_ref.even_ref
  11.4 1.6 %collective-permute-start.3 = (bf16[16,6272]{1,0:T(8,128)(2,1)S(1)}, bf16[16,6272]{1,0:T(8,128)(2,1)S(1)}, u32[]{:S(2)}, u32[]{:S(2)}) collective-permute-start(bf16[16,6272]{1,0:T(8,128)(2,1)S(1)} %join.1.after_ref.even_ref), channel_id=1, source_target_pairs={{0,1},{1,0},{2,3},{3,2},{4,5},{5,4},{6,7},{7,6},{8,9},{9,8},{10,11... | collective-permute-start | bytes 602120 | tf_op jit(solution)/shard_map/ppermute | solution.py:178
  13.0 0.0 collective-permute-start.4
  13.0 2.6 %fetch.1.held_ref = bf16[2560,1024]{1,0:T(8,128)(2,1)S(1)} custom-call(bf16[16,6272]{1,0:T(8,128)(2,1)S(1)} %join.1.after_ref.even_ref, bf16[2560,6144]{1,0:T(8,128)(2,1)} %w_down_ref.3), custom_call_target="tpu_custom_call" | custom-call | bytes 5242880 | tf_op jit(solution)/shard_map/fetch/pallas_call | solution.py:211
  15.6 1.7 %collective-permute-done.3.odd_ref = bf16[16,6272]{1,0:T(8,128)(2,1)S(1)} collective-permute-done((bf16[16,6272]{1,0:T(8,128)(2,1)S(1)}, bf16[16,6272]{1,0:T(8,128)(2,1)S(1)}, u32[]{:S(2)}, u32[]{:S(2)}) %collective-permute-start.3) | collective-permute-done | bytes 200736 | tf_op jit(solution)/shard_map/ppermute | solution.py:178
  17.3 0.0 collective-permute-start.5
  17.3 0.0 collective-permute-done.4.other_even_ref
  17.3 1.4 %collective-permute-done.5.other_odd_ref = bf16[16,6272]{1,0:T(8,128)(2,1)S(1)} collective-permute-done((bf16[16,6272]{1,0:T(8,128)(2,1)S(1)}, bf16[16,6272]{1,0:T(8,128)(2,1)S(1)}, u32[]{:S(2)}, u32[]{:S(2)}) %collective-permute-start.5) | collective-permute-done | bytes 200736 | tf_op jit(solution)/shard_map/ppermute | solution.py:173
  18.8 0.0 slice-done
  18.8 0.0 slice-done.1
  18.8 0.0 slice-done.2
  18.8 0.0 slice-done.3
  18.8 0.0 slice-done.4
  18.8 0.0 slice-done.5
  18.8 0.0 slice-done.6
  18.8 0.0 slice-done.7
  18.8 19.8 %experts.1 = (bf16[16,6144]{1,0:T(8,128)(2,1)S(1)}, bf16[16,6144]{1,0:T(8,128)(2,1)S(1)}, bf16[16,6144]{1,0:T(8,128)(2,1)S(1)}, bf16[16,6144]{1,0:T(8,128)(2,1)S(1)}) custom-call(bf16[16,6272]{1,0:T(8,128)(2,1)S(1)} %join.1.after_ref.even_ref, bf16[16,6272]{1,0:T(8,128)(2,1)S(1)} %collective-permute-done.3.odd_ref, ...), custom_call_target="tpu_custom_call" | custom-call | flops 6039797760 | bytes 57671680 | tf_op jit(solution)/shard_map/experts/pallas_call | solution.py:227
  38.6 0.2 collective-permute-start.7
  38.8 0.4 collective-permute-start.6
  39.2 0.9 %collective-permute-done.7 = bf16[16,6144]{1,0:T(8,128)(2,1)S(1)} collective-permute-done((bf16[16,6144]{1,0:T(8,128)(2,1)S(1)}, bf16[16,6144]{1,0:T(8,128)(2,1)S(1)}, u32[]{:S(2)}, u32[]{:S(2)}) %collective-permute-start.7) | collective-permute-done | bytes 196640 | tf_op jit(solution)/shard_map/ppermute | solution.py:173
  40.1 0.1 add_convert_fusion.1
  40.2 1.6 %collective-permute-start.8 = (bf16[16,6144]{1,0:T(8,128)(2,1)S(1)}, bf16[16,6144]{1,0:T(8,128)(2,1)S(1)}, u32[]{:S(2)}, u32[]{:S(2)}) collective-permute-start(bf16[16,6144]{1,0:T(8,128)(2,1)S(1)} %add_convert_fusion.1), channel_id=1, source_target_pairs={{0,1},{1,0},{2,3},{3,2},{4,5},{5,4},{6,7},{7,6},{8,9},{9,8},{10,11... | collective-permute-start | bytes 589832 | tf_op jit(solution)/shard_map/ppermute | solution.py:178
  41.8 0.0 collective-permute-done.6
  41.8 5.4 %collective-permute-done.8 = bf16[16,6144]{1,0:T(8,128)(2,1)S(1)} collective-permute-done((bf16[16,6144]{1,0:T(8,128)(2,1)S(1)}, bf16[16,6144]{1,0:T(8,128)(2,1)S(1)}, u32[]{:S(2)}, u32[]{:S(2)}) %collective-permute-start.8) | collective-permute-done | bytes 196640 | tf_op jit(solution)/shard_map/ppermute | solution.py:178
  47.2 0.1 add_convert_fusion
  47.3 0.1 fusion
  47.3 0.8 %collective-permute-start.9 = (bf16[4,6144]{1,0:T(4,128)(2,1)S(1)}, bf16[4,6144]{1,0:T(4,128)(2,1)S(1)}, u32[]{:S(2)}, u32[]{:S(2)}) collective-permute-start(bf16[4,6144]{1,0:T(4,128)(2,1)S(1)} %get-tuple-element.17), channel_id=1, source_target_pairs={{0,2},{1,3},{2,0},{3,1},{4,6},{5,7},{6,4},{7,5},{8,10},{9,11},{10,... | collective-permute-start | bytes 147464 | tf_op jit(solution)/shard_map/ppermute | solution.py:178
  48.1 2.6 %collective-permute-start.11 = (bf16[4,6144]{1,0:T(4,128)(2,1)S(1)}, bf16[4,6144]{1,0:T(4,128)(2,1)S(1)}, u32[]{:S(2)}, u32[]{:S(2)}) collective-permute-start(bf16[4,6144]{1,0:T(4,128)(2,1)S(1)} %get-tuple-element.18), channel_id=1, source_target_pairs={{0,6},{1,7},{2,4},{3,5},{4,2},{5,3},{6,0},{7,1},{8,14},{9,15},{10,... | collective-permute-start | bytes 147464 | tf_op jit(solution)/shard_map/ppermute | solution.py:178
  50.7 0.1 collective-permute-start.10
  50.9 0.6 %collective-permute-done.9 = bf16[4,6144]{1,0:T(4,128)(2,1)S(1)} collective-permute-done((bf16[4,6144]{1,0:T(4,128)(2,1)S(1)}, bf16[4,6144]{1,0:T(4,128)(2,1)S(1)}, u32[]{:S(2)}, u32[]{:S(2)}) %collective-permute-start.9) | collective-permute-done | bytes 49184 | tf_op jit(solution)/shard_map/ppermute | solution.py:178
  51.5 2.6 %collective-permute-done.11 = bf16[4,6144]{1,0:T(4,128)(2,1)S(1)} collective-permute-done((bf16[4,6144]{1,0:T(4,128)(2,1)S(1)}, bf16[4,6144]{1,0:T(4,128)(2,1)S(1)}, u32[]{:S(2)}, u32[]{:S(2)}) %collective-permute-start.11) | collective-permute-done | bytes 49184 | tf_op jit(solution)/shard_map/ppermute | solution.py:178
  54.1 1.6 %collective-permute-done.10 = bf16[4,6144]{1,0:T(4,128)(2,1)S(1)} collective-permute-done((bf16[4,6144]{1,0:T(4,128)(2,1)S(1)}, bf16[4,6144]{1,0:T(4,128)(2,1)S(1)}, u32[]{:S(2)}, u32[]{:S(2)}) %collective-permute-start.10) | collective-permute-done | bytes 49184 | tf_op jit(solution)/shard_map/ppermute | solution.py:178
  55.7 0.7 %add_convert_fusion.2 = bf16[4,6144]{1,0:T(4,128)(2,1)} fusion(bf16[4,6144]{1,0:T(4,128)(2,1)S(1)} %collective-permute-done.11, bf16[4,6144]{1,0:T(4,128)(2,1)S(1)} %collective-permute-done.10, bf16[4,6144]{1,0:T(4,128)(2,1)S(1)} %collective-permute-done.9, bf16[16,6144]{1,0:T(8,128)(2,1)S(1)} %add_convert_fusion), kind=kLoop, calls=%fused_computation.2 | loop fusion | flops 196608 | bytes 245760 | tf_op jit(solution)/shard_map/convert_element_type | solution.py:264
  (1 shorter events, 0.0 us)
Async XLA Ops:
  0.0 18.8 %slice-start = ((s8[31457280]{0:T(1024)(128)(4,1)}), s8[4194304]{0:T(1024)(128)(4,1)S(1)}, s32[]{:S(2)}) async-start(s8[31457280]{0:T(1024)(128)(4,1)} %bitcast.2), calls=%async_computation | async-start | bytes 8388608
  0.0 18.8 %slice-start.1 = ((s8[31457280]{0:T(1024)(128)(4,1)}), s8[4194304]{0:T(1024)(128)(4,1)S(1)}, s32[]{:S(2)}) async-start(s8[31457280]{0:T(1024)(128)(4,1)} %bitcast.2), calls=%async_computation.1 | async-start | bytes 8388608
  0.0 18.8 %slice-start.2 = ((s8[31457280]{0:T(1024)(128)(4,1)}), s8[4194304]{0:T(1024)(128)(4,1)S(1)}, s32[]{:S(2)}) async-start(s8[31457280]{0:T(1024)(128)(4,1)} %bitcast.2), calls=%async_computation.2 | async-start | bytes 8388608
  0.0 18.8 %slice-start.3 = ((s8[31457280]{0:T(1024)(128)(4,1)}), s8[4194304]{0:T(1024)(128)(4,1)S(1)}, s32[]{:S(2)}) async-start(s8[31457280]{0:T(1024)(128)(4,1)} %bitcast.2), calls=%async_computation.3 | async-start | bytes 8388608
  0.0 18.8 %slice-start.4 = ((s8[31457280]{0:T(1024)(128)(4,1)}), s8[4194304]{0:T(1024)(128)(4,1)S(1)}, s32[]{:S(2)}) async-start(s8[31457280]{0:T(1024)(128)(4,1)} %bitcast.2), calls=%async_computation.4 | async-start | bytes 8388608
  0.0 18.8 %slice-start.5 = ((s8[31457280]{0:T(1024)(128)(4,1)}), s8[4194304]{0:T(1024)(128)(4,1)S(1)}, s32[]{:S(2)}) async-start(s8[31457280]{0:T(1024)(128)(4,1)} %bitcast.2), calls=%async_computation.5 | async-start | bytes 8388608
  0.0 18.8 %slice-start.6 = ((s8[31457280]{0:T(1024)(128)(4,1)}), s8[4194304]{0:T(1024)(128)(4,1)S(1)}, s32[]{:S(2)}) async-start(s8[31457280]{0:T(1024)(128)(4,1)} %bitcast.2), calls=%async_computation.6 | async-start | bytes 8388608
  0.0 18.8 %slice-start.7 = ((s8[31457280]{0:T(1024)(128)(4,1)}), s8[2097152]{0:T(1024)(128)(4,1)S(1)}, s32[]{:S(2)}) async-start(s8[31457280]{0:T(1024)(128)(4,1)} %bitcast.2), calls=%async_computation.7 | async-start | bytes 4194304
  1.2 7.4 %collective-permute-start.2 = (bf16[4,6272]{1,0:T(4,128)(2,1)S(1)}, bf16[4,6272]{1,0:T(4,128)(2,1)S(1)}, u32[]{:S(2)}, u32[]{:S(2)}) collective-permute-start(bf16[4,6272]{1,0:T(4,128)(2,1)S(1)} %norm.1.refs_0_), channel_id=1, source_target_pairs={{0,6},{1,7},{2,4},{3,5},{4,2},{5,3},{6,0},{7,1},{8,14},{9,15},{10,... | collective-permute-start | bytes 150536 | tf_op jit(solution)/shard_map/ppermute | solution.py:178
  6.3 5.0 %collective-permute-start.1 = (bf16[4,6272]{1,0:T(4,128)(2,1)S(1)}, bf16[4,6272]{1,0:T(4,128)(2,1)S(1)}, u32[]{:S(2)}, u32[]{:S(2)}) collective-permute-start(bf16[4,6272]{1,0:T(4,128)(2,1)S(1)} %norm.1.refs_0_), channel_id=1, source_target_pairs={{0,4},{1,5},{2,6},{3,7},{4,0},{5,1},{6,2},{7,3},{8,12},{9,13},{10,... | collective-permute-start | bytes 150536 | tf_op jit(solution)/shard_map/ppermute | solution.py:178
  6.3 5.0 %collective-permute-start = (bf16[4,6272]{1,0:T(4,128)(2,1)S(1)}, bf16[4,6272]{1,0:T(4,128)(2,1)S(1)}, u32[]{:S(2)}, u32[]{:S(2)}) collective-permute-start(bf16[4,6272]{1,0:T(4,128)(2,1)S(1)} %norm.1.refs_0_), channel_id=1, source_target_pairs={{0,2},{1,3},{2,0},{3,1},{4,6},{5,7},{6,4},{7,5},{8,10},{9,11},{10,... | collective-permute-start | bytes 150536 | tf_op jit(solution)/shard_map/ppermute | solution.py:178
  11.4 5.9 %collective-permute-start.3 = (bf16[16,6272]{1,0:T(8,128)(2,1)S(1)}, bf16[16,6272]{1,0:T(8,128)(2,1)S(1)}, u32[]{:S(2)}, u32[]{:S(2)}) collective-permute-start(bf16[16,6272]{1,0:T(8,128)(2,1)S(1)} %join.1.after_ref.even_ref), channel_id=1, source_target_pairs={{0,1},{1,0},{2,3},{3,2},{4,5},{5,4},{6,7},{7,6},{8,9},{9,8},{10,11... | collective-permute-start | bytes 602120 | tf_op jit(solution)/shard_map/ppermute | solution.py:178
  13.0 4.3 %collective-permute-start.4 = (bf16[16,6272]{1,0:T(8,128)(2,1)S(1)}, bf16[16,6272]{1,0:T(8,128)(2,1)S(1)}, u32[]{:S(2)}, u32[]{:S(2)}) collective-permute-start(bf16[16,6272]{1,0:T(8,128)(2,1)S(1)} %join.1.after_ref.even_ref), channel_id=1, source_target_pairs={{0,8},{8,0},{1,9},{9,1},{2,10},{10,2},{3,11},{11,3},{4,12},{12,4},... | collective-permute-start | bytes 602120 | tf_op jit(solution)/shard_map/ppermute | solution.py:173
  17.3 1.4 %collective-permute-start.5 = (bf16[16,6272]{1,0:T(8,128)(2,1)S(1)}, bf16[16,6272]{1,0:T(8,128)(2,1)S(1)}, u32[]{:S(2)}, u32[]{:S(2)}) collective-permute-start(bf16[16,6272]{1,0:T(8,128)(2,1)S(1)} %collective-permute-done.3.odd_ref), channel_id=1, source_target_pairs={{0,8},{8,0},{1,9},{9,1},{2,10},{10,2},{3,11},{11,3},{4,12},{12,4},... | collective-permute-start | bytes 602120 | tf_op jit(solution)/shard_map/ppermute | solution.py:173
  38.6 1.5 %collective-permute-start.7 = (bf16[16,6144]{1,0:T(8,128)(2,1)S(1)}, bf16[16,6144]{1,0:T(8,128)(2,1)S(1)}, u32[]{:S(2)}, u32[]{:S(2)}) collective-permute-start(bf16[16,6144]{1,0:T(8,128)(2,1)S(1)} %get-tuple-element.16), channel_id=1, source_target_pairs={{0,8},{8,0},{1,9},{9,1},{2,10},{10,2},{3,11},{11,3},{4,12},{12,4},... | collective-permute-start | bytes 589832 | tf_op jit(solution)/shard_map/ppermute | solution.py:173
  38.8 3.0 %collective-permute-start.6 = (bf16[16,6144]{1,0:T(8,128)(2,1)S(1)}, bf16[16,6144]{1,0:T(8,128)(2,1)S(1)}, u32[]{:S(2)}, u32[]{:S(2)}) collective-permute-start(bf16[16,6144]{1,0:T(8,128)(2,1)S(1)} %get-tuple-element.14), channel_id=1, source_target_pairs={{0,8},{8,0},{1,9},{9,1},{2,10},{10,2},{3,11},{11,3},{4,12},{12,4},... | collective-permute-start | bytes 589832 | tf_op jit(solution)/shard_map/ppermute | solution.py:173
  40.2 7.0 %collective-permute-start.8 = (bf16[16,6144]{1,0:T(8,128)(2,1)S(1)}, bf16[16,6144]{1,0:T(8,128)(2,1)S(1)}, u32[]{:S(2)}, u32[]{:S(2)}) collective-permute-start(bf16[16,6144]{1,0:T(8,128)(2,1)S(1)} %add_convert_fusion.1), channel_id=1, source_target_pairs={{0,1},{1,0},{2,3},{3,2},{4,5},{5,4},{6,7},{7,6},{8,9},{9,8},{10,11... | collective-permute-start | bytes 589832 | tf_op jit(solution)/shard_map/ppermute | solution.py:178
  47.3 4.2 %collective-permute-start.9 = (bf16[4,6144]{1,0:T(4,128)(2,1)S(1)}, bf16[4,6144]{1,0:T(4,128)(2,1)S(1)}, u32[]{:S(2)}, u32[]{:S(2)}) collective-permute-start(bf16[4,6144]{1,0:T(4,128)(2,1)S(1)} %get-tuple-element.17), channel_id=1, source_target_pairs={{0,2},{1,3},{2,0},{3,1},{4,6},{5,7},{6,4},{7,5},{8,10},{9,11},{10,... | collective-permute-start | bytes 147464 | tf_op jit(solution)/shard_map/ppermute | solution.py:178
  48.1 6.0 %collective-permute-start.11 = (bf16[4,6144]{1,0:T(4,128)(2,1)S(1)}, bf16[4,6144]{1,0:T(4,128)(2,1)S(1)}, u32[]{:S(2)}, u32[]{:S(2)}) collective-permute-start(bf16[4,6144]{1,0:T(4,128)(2,1)S(1)} %get-tuple-element.18), channel_id=1, source_target_pairs={{0,6},{1,7},{2,4},{3,5},{4,2},{5,3},{6,0},{7,1},{8,14},{9,15},{10,... | collective-permute-start | bytes 147464 | tf_op jit(solution)/shard_map/ppermute | solution.py:178
  50.7 5.0 %collective-permute-start.10 = (bf16[4,6144]{1,0:T(4,128)(2,1)S(1)}, bf16[4,6144]{1,0:T(4,128)(2,1)S(1)}, u32[]{:S(2)}, u32[]{:S(2)}) collective-permute-start(bf16[4,6144]{1,0:T(4,128)(2,1)S(1)} %get-tuple-element.19), channel_id=1, source_target_pairs={{0,4},{1,5},{2,6},{3,7},{4,0},{5,1},{6,2},{7,3},{8,12},{9,13},{10,... | collective-permute-start | bytes 147464 | tf_op jit(solution)/shard_map/ppermute | solution.py:178
